TPU v7x, 32 devices: a whole 2x2x4 slice. The times are simulated.
32 devices in a mesh: span: 8 (over z, core), chord: 4 (over y, x).
Axes of the slice: x: 2, y: 2, z: 4, core: 2. Of those that a mesh axis runs over, the one named last changes fastest.
Arguments:
- flow_state: float32 [2, 5, 32, 256, 128], P(None, None, 'span', 'chord'), may hold values from -6 to 6
- jacobians: bfloat16 [7, 5, 5, 32, 256, 128], P(None, None, None, 'span', 'chord'), may hold values from -1 to 1
- beam_state: float32 [2, 12, 2048], P(None, None, 'span'), may hold values from -6 to 6
- stiffness: float32 [5, 12, 12, 2048], P(None, None, None, 'span'), may hold values from -0.75 to 0.75
- motion_map: float32 [5, 12, 32, 256], P(None, None, 'span', 'chord'), may hold values from -1.75 to 1.75
- load_map: float32 [12, 5, 32, 256], P(None, None, 'span', 'chord'), may hold values from -2.5 to 2.5
- surface_mask: int32 [32, 256], P('span', 'chord'), may hold values 0 or 1
- station_of: int32 [32, 256], P('span', 'chord'), may hold values from 0 to 2047
Outputs:
- flow_image: float32 [2, 5, 32, 256, 128], P(None, None, 'span', 'chord')
- beam_image: float32 [2, 12, 2048], P(None, None, 'span')
All inputs are finite; a program needn't handle non-finite values. No bound on the sum of `surface_mask` on one device may be relied on, other than what follows from the above.
Results may differ from a plain program's by a relative error of at most 0.0003.
Values sent between devices are 32-bit elements; how exact they have to be, the bound alone decides.
No kernel may reach another device: no remote copies, remote signals or barrier semaphores. Data moves between devices by JAX's collectives and lax.ppermute only.
A program may use at most 192 MiB of HBM per device.

v0:
```python
import functools

import jax
import jax.numpy as jnp
from jax import lax
from jax.experimental import pallas as pl
from jax.experimental.pallas import tpu as pltpu
from jax.sharding import PartitionSpec as P

F32 = jnp.float32
BF16 = jnp.bfloat16
LANES = 128
VMEM = pl.BlockSpec(memory_space=pltpu.VMEM)
LIMIT = 48 * 1024 * 1024


def params():
    return pltpu.CompilerParams(vmem_limit_bytes=LIMIT)


def halves(x):
    hi = x.astype(BF16).astype(F32)
    return jnp.concatenate([hi, x - hi], axis=0).astype(BF16)


def lane_row(x, width):
    return jnp.concatenate([x[r : r + 1, :width] for r in range(x.shape[0])], axis=1)


def table(stations, first, count):
    rows = lax.broadcasted_iota(jnp.int32, (count, stations.shape[1]), 0) + first
    return (rows == stations).astype(F32).astype(BF16)


def put_slabs(ref, base, rows):
    n = rows.shape[0]
    for h in range(rows.shape[1] // LANES):
        ref[base + h * n : base + (h + 1) * n] = rows[:, h * LANES : (h + 1) * LANES]


def get_slabs(ref, base, n, k):
    return jnp.concatenate([ref[base + h * n : base + (h + 1) * n] for h in range(k)], axis=1)


def relative(sta, me, sta_dev, ccols):
    return lane_row(sta[...] ^ (me * sta_dev), ccols)


def pre_kernel(span, flow, lmap, mask, sta, beam, p1, far, up, down, kept, wall):
    nvec, nvar, srows, ccols, _ = flow.shape
    ndof, _, sta_dev = beam.shape
    k = sta_dev // LANES
    rows = nvec * ndof
    halo = nvec * nvar * ccols
    me = lax.axis_index("span")
    near_row = jnp.where(me % 2 == 1, 0, srows - 1)
    far_row = srows - 1 - near_row
    lane = lax.broadcasted_iota(jnp.int32, (ccols, LANES), 1)
    packed = jnp.zeros((ccols, LANES), F32)
    for v in range(nvec):
        for b in range(nvar):
            q = v * nvar + b
            p1[q * ccols : (q + 1) * ccols] = flow[v, b, near_row]
            far[q * ccols : (q + 1) * ccols] = flow[v, b, far_row]
            up[q] = flow[v, b, :, ccols - 1, :]
            down[q] = flow[v, b, :, 0, :]
            for r in range(srows):
                at = q * 8 + r
                x = flow[v, b, r]
                if at:
                    x = pltpu.roll(x, at, 1)
                packed = jnp.where(lane == at, x, packed)
    surf = packed.T
    maskf = mask[...].astype(F32)
    for v in range(nvec):
        near = [surf[(v * nvar + a) * 8 : (v * nvar + a) * 8 + srows] * maskf for a in range(nvar)]
        for j in range(ndof):
            total = lmap[j, 0] * near[0]
            for a in range(1, nvar):
                total = total + lmap[j, a] * near[a]
            wall[v * ndof + j] = total
    walls = jnp.concatenate([wall[:, r, :] for r in range(srows)], axis=1)
    parts = halves(walls)
    stations = relative(sta, me, sta_dev, ccols)
    for p in range(span):
        both = lax.dot_general(
            parts,
            table(stations, p * sta_dev, sta_dev),
            (((1,), (1,)), ((), ())),
            preferred_element_type=F32,
        )
        term = both[:rows] + both[rows:]
        if p % 2:
            put_slabs(p1, halo + (p // 2) * rows * k, term)
        else:
            put_slabs(kept, (p // 2) * rows * k, term)
    base = halo + (span // 2) * rows * k
    for v in range(nvec):
        for j in range(ndof):
            for h in range(k):
                at = base + h * rows + v * ndof + j
                p1[at : at + 1] = beam[j, v : v + 1, h * LANES : (h + 1) * LANES]


def combine_kernel(halo, slab, sent, got, kept, own, *out):
    groups = len(out) + 1
    base = halo + groups * slab
    own[...] = kept[:slab] + got[halo : halo + slab]
    for q in range(1, groups):
        o = out[q - 1]
        o[:slab] = kept[q * slab : (q + 1) * slab] + got[halo + q * slab : halo + (q + 1) * slab]
        o[slab : 2 * slab] = sent[base : base + slab]
        o[2 * slab :] = got[base : base + slab]


def stencil_kernel(flow, jac, got, lo, hi, out, near):
    nvec, nvar, srows, ccols, _ = flow.shape
    r = pl.program_id(0)
    me = lax.axis_index("span")
    odd = me % 2
    row = lax.broadcasted_iota(jnp.int32, (ccols, LANES), 0)
    lane = lax.broadcasted_iota(jnp.int32, (ccols, LANES), 1)
    for v in range(nvec):
        for b in range(nvar):
            q = v * nvar + b
            x = flow[v, b, r]
            near[0, q] = jnp.where(row == 0, lo[q, pl.ds(r, 1)], pltpu.roll(x, 1, 0))
            near[1, q] = jnp.where(row == ccols - 1, hi[q, pl.ds(r, 1)], pltpu.roll(x, ccols - 1, 0))
            near[2, q] = jnp.where(lane == 0, 0.0, pltpu.roll(x, 1, 1))
            near[3, q] = jnp.where(lane == LANES - 1, 0.0, pltpu.roll(x, LANES - 1, 1))
    first, last = r == 0, r == srows - 1
    below = jnp.where(first, 0, r - 1)
    above = jnp.where(last, srows - 1, r + 1)
    low_on = jnp.where(odd == 1, 1.0, 0.0).astype(F32)
    high_on = 1.0 - low_on
    tile = 16

    def body(t, carry):
        c = pl.multiple_of(t * tile, tile)
        here = pl.ds(c, tile)
        acc = [[jnp.zeros((tile, LANES), F32) for _ in range(nvar)] for _ in range(nvec)]
        for e in range(7):
            for b in range(nvar):
                xs = []
                for v in range(nvec):
                    q = v * nvar + b
                    if e == 0:
                        x = flow[v, b, r, here]
                    elif e == 1:
                        h = got[pl.ds(q * ccols + c, tile)] * low_on
                        x = jnp.where(first, h, flow[v, b, below, here])
                    elif e == 2:
                        h = got[pl.ds(q * ccols + c, tile)] * high_on
                        x = jnp.where(last, h, flow[v, b, above, here])
                    else:
                        x = near[e - 3, q, here]
                    xs.append(x)
                for a in range(nvar):
                    m = jac[e, a, b, 0, here].astype(F32)
                    for v in range(nvec):
                        acc[v][a] = acc[v][a] + m * xs[v]
        for v in range(nvec):
            for a in range(nvar):
                out[v, a, 0, here] = acc[v][a]
        return carry

    lax.fori_loop(0, ccols // tile, body, 0)


def couple_kernel(
    span, flow_in, jac, far, motion, mask, sta, stiff, sent, got, *rest
):
    groups = span // 2
    zs = rest[: groups - 1]
    flow, band, gath, lk, block, sem = rest[groups - 1 :]
    nvec, nvar, srows, ccols, _ = flow_in.shape
    _, ndof, _, sta_dev = stiff.shape
    k = sta_dev // LANES
    rows = nvec * ndof
    slab = rows * k
    halo = nvec * nvar * ccols
    me = lax.axis_index("span")
    odd = me % 2
    e = 1 + odd
    r_far = jnp.where(odd == 1, srows - 1, 0)
    fetch = pltpu.make_async_copy(jac.at[e, :, :, r_far], block, sem)
    fetch.start()
    base = halo + groups * slab
    gath[0] = get_slabs(sent, base, rows, k)
    gath[1] = get_slabs(got, base, rows, k)
    for q in range(1, groups):
        gath[2 * q] = get_slabs(zs[q - 1], slab, rows, k)
        gath[2 * q + 1] = get_slabs(zs[q - 1], 2 * slab, rows, k)
    stations = relative(sta, me, sta_dev, ccols)
    both = jnp.zeros((2 * rows, srows * ccols), F32)
    for p in range(span):
        both = both + jnp.dot(
            halves(gath[p]), table(stations, p * sta_dev, sta_dev), preferred_element_type=F32
        )
    looked = both[:rows] + both[rows:]
    for r in range(srows):
        lk[:, r, :] = looked[:, r * ccols : (r + 1) * ccols]
    maskf = mask[...].astype(F32)
    tiles = []
    for v in range(nvec):
        for a in range(nvar):
            total = motion[a, 0] * lk[v * ndof]
            for j in range(1, ndof):
                total = total + motion[a, j] * lk[v * ndof + j]
            total = total * maskf
            tiles.append(jnp.concatenate([total, jnp.zeros((8 - srows, ccols), F32)], axis=0))
    tiles.append(jnp.zeros((LANES - 8 * len(tiles), ccols), F32))
    packed = jnp.concatenate(tiles, axis=0).T
    lane = lax.broadcasted_iota(jnp.int32, (ccols, LANES), 1)
    for v in range(nvec):
        for a in range(nvar):
            for r in range(srows):
                at = (v * nvar + a) * 8 + r
                x = packed if at == 0 else pltpu.roll(packed, LANES - at, 1)
                flow[v, a, r] = flow_in[v, a, r] + jnp.where(lane == 0, x, 0.0)
    own = gath[0]
    before = gath[jnp.where(me > 0, me ^ (me - 1), 0)]
    after = gath[jnp.where(me < span - 1, me ^ (me + 1), 0)]
    pos = lax.broadcasted_iota(jnp.int32, (rows, sta_dev), 1)
    place = pos + me * sta_dev
    stations_all = span * sta_dev
    blade_len = stations_all // 4

    def blade(t):
        n = jnp.zeros(t.shape, jnp.int32)
        for m in range(1, 5):
            n = n + (t + sta_dev // 2 >= m * blade_len).astype(jnp.int32)
        return n

    home = blade(place)
    shifted = []
    for d in range(5):
        s = d - 2
        other = place + s
        x = own if s == 0 else pltpu.roll(own, (-s) % sta_dev, 1)
        if s < 0:
            x = jnp.where(pos < -s, pltpu.roll(before, -s, 1), x)
        if s > 0:
            x = jnp.where(pos >= sta_dev - s, pltpu.roll(after, sta_dev - s, 1), x)
        good = (blade(other) == home) & (other >= 0) & (other < stations_all)
        x = jnp.where(good, x, 0.0)
        shifted.append([x[v * ndof : (v + 1) * ndof] for v in range(nvec)])
    for i in range(ndof):
        for v in range(nvec):
            total = stiff[0, i] * shifted[0][v]
            for d in range(1, 5):
                total = total + stiff[d, i] * shifted[d][v]
            band[i, v : v + 1, :] = jnp.sum(total, axis=0, keepdims=True)
    fetch.wait()
    tile = 16

    def body(t, carry):
        c = pl.multiple_of(t * tile, tile)
        here = pl.ds(c, tile)
        acc = [[flow[v, a, r_far, here] for a in range(nvar)] for v in range(nvec)]
        for b in range(nvar):
            xs = [far[pl.ds((v * nvar + b) * ccols + c, tile)] for v in range(nvec)]
            for a in range(nvar):
                m = block[a, b, here].astype(F32)
                for v in range(nvec):
                    acc[v][a] = acc[v][a] + m * xs[v]
        for v in range(nvec):
            for a in range(nvar):
                flow[v, a, r_far, here] = acc[v][a]
        return carry

    lax.fori_loop(0, ccols // tile, body, 0)


def last_kernel(band, *rest):
    parts, out = rest[:-1], rest[-1]
    ndof, nvec, sta_dev = band.shape
    rows = ndof * nvec
    total = parts[0][...]
    for p in parts[1:]:
        total = total + p[...]
    for v in range(nvec):
        for j in range(ndof):
            for h in range(sta_dev // LANES):
                at = h * rows + v * ndof + j
                cols = slice(h * LANES, (h + 1) * LANES)
                out[j, v : v + 1, cols] = band[j, v : v + 1, cols] - total[at : at + 1]


def reduce_kernel(own, *rest):
    parts, out = rest[:-1], rest[-1]
    total = own[...]
    for p in parts:
        total = total + p[: total.shape[0]]
    out[...] = total


def swap(x, axis, m):
    return lax.ppermute(x, axis, [(i, i ^ m) for i in range(lax.axis_size(axis))])


def on_device(
    flow_state, jacobians, beam_state, stiffness, motion_map, load_map, surface_mask, station_of
):
    nvec, nvar, srows, ccols, ncell = flow_state.shape
    ndof, sta_dev = beam_state.shape[1:]
    span, chord = lax.axis_size("span"), lax.axis_size("chord")
    groups = span // 2
    k = sta_dev // LANES
    rows = nvec * ndof
    slab = rows * k
    halo = nvec * nvar * ccols
    nq = nvec * nvar
    beam = jnp.transpose(beam_state, (1, 0, 2))

    def shape(*s):
        return jax.ShapeDtypeStruct(s, F32)

    p1, far, up, down, kept = pl.pallas_call(
        functools.partial(pre_kernel, span),
        out_shape=(
            shape(halo + (groups + 1) * slab, LANES),
            shape(halo, LANES),
            shape(nq, srows, LANES),
            shape(nq, srows, LANES),
            shape(groups * slab, LANES),
        ),
        in_specs=[VMEM] * 5,
        out_specs=(VMEM,) * 5,
        scratch_shapes=[pltpu.VMEM((rows, srows, ccols), F32)],
        compiler_params=params(),
        name="pre",
    )(flow_state, load_map, surface_mask, station_of, beam)

    pairs = []
    for i in range(1, span - 1, 2):
        pairs += [(i, i + 1), (i + 1, i)]
    far_got = lax.ppermute(far, "span", pairs)
    lo = lax.ppermute(up, "chord", [(i, i + 1) for i in range(chord - 1)])
    hi = lax.ppermute(down, "chord", [(i + 1, i) for i in range(chord - 1)])
    p1_got = swap(p1, "span", 1)

    own, *zs = pl.pallas_call(
        functools.partial(combine_kernel, halo, slab),
        out_shape=(shape(slab, LANES),) + (shape(3 * slab, LANES),) * (groups - 1),
        in_specs=[VMEM] * 3,
        out_specs=(VMEM,) * groups,
        compiler_params=params(),
        name="combine",
    )(p1, p1_got, kept)
    z_got = [swap(zs[q - 1], "span", 2 * q) for q in range(1, groups)]

    whole = pl.BlockSpec(flow_state.shape, lambda r: (0, 0, 0, 0, 0))
    flow1 = pl.pallas_call(
        stencil_kernel,
        grid=(srows,),
        out_shape=jax.ShapeDtypeStruct(flow_state.shape, F32),
        in_specs=[
            whole,
            pl.BlockSpec((7, nvar, nvar, 1, ccols, ncell), lambda r: (0, 0, 0, r, 0, 0)),
            pl.BlockSpec(p1_got.shape, lambda r: (0, 0)),
            pl.BlockSpec(lo.shape, lambda r: (0, 0, 0)),
            pl.BlockSpec(hi.shape, lambda r: (0, 0, 0)),
        ],
        out_specs=pl.BlockSpec((nvec, nvar, 1, ccols, ncell), lambda r: (0, 0, r, 0, 0)),
        scratch_shapes=[pltpu.VMEM((4, nq, ccols, LANES), F32)],
        compiler_params=params(),
        cost_estimate=pl.CostEstimate(
            flops=4 * 7 * nvar * nvar * srows * ccols * ncell,
            bytes_accessed=2 * jacobians.size + 8 * flow_state.size,
            transcendentals=0,
        ),
        name="stencil",
    )(flow_state, jacobians, p1_got, lo, hi)

    loads = pl.pallas_call(
        reduce_kernel,
        out_shape=shape(slab, LANES),
        in_specs=[VMEM] * groups,
        out_specs=VMEM,
        compiler_params=params(),
        name="reduce",
    )(own, *z_got)
    chord_got = [swap(loads, "chord", m) for m in range(1, chord)]

    flow_image, band = pl.pallas_call(
        functools.partial(couple_kernel, span),
        out_shape=(jax.ShapeDtypeStruct(flow_state.shape, F32), shape(ndof, nvec, sta_dev)),
        in_specs=[VMEM, pl.BlockSpec(memory_space=pl.ANY)] + [VMEM] * (7 + groups - 1),
        out_specs=(VMEM, VMEM),
        scratch_shapes=[
            pltpu.VMEM((span, rows, sta_dev), F32),
            pltpu.VMEM((rows, srows, ccols), F32),
            pltpu.VMEM((nvar, nvar, ccols, ncell), BF16),
            pltpu.SemaphoreType.DMA,
        ],
        compiler_params=params(),
        cost_estimate=pl.CostEstimate(flops=20000000, bytes_accessed=6000000, transcendentals=0),
        name="couple",
    )(
        flow1, jacobians, far_got, motion_map, surface_mask, station_of, stiffness, p1, p1_got, *z_got
    )

    out = pl.pallas_call(
        last_kernel,
        out_shape=shape(ndof, nvec, sta_dev),
        in_specs=[VMEM] * (chord + 1),
        out_specs=VMEM,
        compiler_params=params(),
        name="last",
    )(band, loads, *chord_got)
    return flow_image, jnp.transpose(out, (1, 0, 2))


def solution(mesh):
    in_specs = (
        P(None, None, "span", "chord", None),
        P(None, None, None, "span", "chord", None),
        P(None, None, "span"),
        P(None, None, None, "span"),
        P(None, None, "span", "chord"),
        P(None, None, "span", "chord"),
        P("span", "chord"),
        P("span", "chord"),
    )
    out_specs = (P(None, None, "span", "chord", None), P(None, None, "span"))
    return jax.shard_map(
        on_device, mesh=mesh, in_specs=in_specs, out_specs=out_specs, check_vma=False
    )
```

profile of v0, /device:TPU:0, one launch (start us, length us, event | category | flops | bytes accessed | tf_op | source)
XLA Modules:
  0.0 39.8 jit_solution(2385104603339548342)
XLA Ops:
  0.6 1.3 %copy-done = f32[2,5,4,64,128]{4,3,2,1,0:T(8,128)S(1)} copy-done((f32[2,5,4,64,128]{4,3,2,1,0:T(8,128)S(1)}, f32[2,5,4,64,128]{4,3,2,1,0:T(8,128)}, u32[]{:S(2)}) %copy-start) | copy-done | bytes 1310744
  2.0 0.9 %copy-done.4 = f32[12,5,4,64]{3,2,1,0:T(4,128)S(1)} copy-done((f32[12,5,4,64]{3,2,1,0:T(4,128)S(1)}, f32[12,5,4,64]{3,2,1,0:T(4,128)}, u32[]{:S(2)}) %copy-start.4) | copy-done | bytes 61464
  2.9 0.7 %copy-done.5 = f32[2,12,256]{2,0,1:T(2,128)S(1)} copy-done((f32[2,12,256]{2,0,1:T(2,128)S(1)}, f32[2,12,256]{2,0,1:T(2,128)}, u32[]{:S(2)}) %copy-start.5) | copy-done | bytes 24600
  3.6 0.7 %copy-done.6 = s32[4,64]{1,0:T(4,128)S(1)} copy-done((s32[4,64]{1,0:T(4,128)S(1)}, s32[4,64]{1,0:T(4,128)}, u32[]{:S(2)}) %copy-start.6) | copy-done | bytes 1048
  4.3 0.7 %copy-done.7 = s32[4,64]{1,0:T(4,128)S(1)} copy-done((s32[4,64]{1,0:T(4,128)S(1)}, s32[4,64]{1,0:T(4,128)}, u32[]{:S(2)}) %copy-start.7) | copy-done | bytes 1048
  5.0 0.9 %pre.1 = (f32[880,128]{1,0:T(8,128)S(1)}, f32[640,128]{1,0:T(8,128)S(1)}, f32[10,4,128]{2,1,0:T(4,128)S(1)}, f32[10,4,128]{2,1,0:T(4,128)S(1)}, f32[192,128]{1,0:T(8,128)S(1)}) custom-call(f32[2,5,4,64,128]{4,3,2,1,0:T(8,128)S(1)} %copy-done, f32[12,5,4,64]{3,2,1,0:T(4,128)S(1)} %copy-done.4, s32[4,64]{1,0:T(4,128)S(1)} %copy-done.6, s32[4,64]{1,0:T(4,128)S(1)} %copy-done.7, ...), custom_call_target="tpu_custom_call" | custom-call | tf_op jit(solution)/shard_map/pre/pallas_call | solution.py:319
  5.9 0.5 %collective-permute-start = (f32[880,128]{1,0:T(8,128)S(1)}, f32[880,128]{1,0:T(8,128)S(1)}, u32[]{:S(2)}, u32[]{:S(2)}) collective-permute-start(f32[880,128]{1,0:T(8,128)S(1)} %get-tuple-element.13.sent), channel_id=1, source_target_pairs={{0,4},{4,0},{8,12},{12,8},{16,20},{20,16},{24,28},{28,24},{1,5},{5... | collective-permute-start | bytes 1351688 | tf_op jit(solution)/shard_map/ppermute | solution.py:299
  6.4 0.7 %collective-permute-start.3 = (f32[640,128]{1,0:T(8,128)S(1)}, f32[640,128]{1,0:T(8,128)S(1)}, u32[]{:S(2)}, u32[]{:S(2)}) collective-permute-start(f32[640,128]{1,0:T(8,128)S(1)} %get-tuple-element.16), channel_id=1, source_target_pairs={{4,8},{8,4},{12,16},{16,12},{20,24},{24,20},{5,9},{9,5},{13,17},{1... | collective-permute-start | bytes 983048 | tf_op jit(solution)/shard_map/ppermute | solution.py:338
  7.1 0.8 %collective-permute-done.got = f32[880,128]{1,0:T(8,128)S(1)} collective-permute-done((f32[880,128]{1,0:T(8,128)S(1)}, f32[880,128]{1,0:T(8,128)S(1)}, u32[]{:S(2)}, u32[]{:S(2)}) %collective-permute-start) | collective-permute-done | bytes 450592 | tf_op jit(solution)/shard_map/ppermute | solution.py:299
  7.9 3.2 %collective-permute-start.4 = (f32[144,128]{1,0:T(8,128)S(1)}, f32[144,128]{1,0:T(8,128)S(1)}, u32[]{:S(2)}, u32[]{:S(2)}) collective-permute-start(f32[144,128]{1,0:T(8,128)S(1)} %get-tuple-element.18), channel_id=1, source_target_pairs={{0,8},{4,12},{8,0},{12,4},{16,24},{20,28},{24,16},{28,20},{1,9},{5... | collective-permute-start | bytes 221192 | tf_op jit(solution)/shard_map/ppermute | solution.py:299
  11.0 3.1 %collective-permute-start.5 = (f32[144,128]{1,0:T(8,128)S(1)}, f32[144,128]{1,0:T(8,128)S(1)}, u32[]{:S(2)}, u32[]{:S(2)}) collective-permute-start(f32[144,128]{1,0:T(8,128)S(1)} %get-tuple-element.19), channel_id=1, source_target_pairs={{0,16},{4,20},{8,24},{12,28},{16,0},{20,4},{24,8},{28,12},{1,17},{... | collective-permute-start | bytes 221192 | tf_op jit(solution)/shard_map/ppermute | solution.py:299
  14.1 3.4 %collective-permute-start.1 = (f32[10,4,128]{2,1,0:T(4,128)S(1)}, f32[10,4,128]{2,1,0:T(4,128)S(1)}, u32[]{:S(2)}, u32[]{:S(2)}) collective-permute-start(f32[10,4,128]{2,1,0:T(4,128)S(1)} %get-tuple-element.14), channel_id=1, source_target_pairs={{0,1},{1,2},{2,3},{4,5},{5,6},{6,7},{8,9},{9,10},{10,11},{12,13},{... | collective-permute-start | bytes 61448 | tf_op jit(solution)/shard_map/ppermute | solution.py:339
  17.5 0.8 %collective-permute-done.4.rest_0_ = f32[144,128]{1,0:T(8,128)S(1)} collective-permute-done((f32[144,128]{1,0:T(8,128)S(1)}, f32[144,128]{1,0:T(8,128)S(1)}, u32[]{:S(2)}, u32[]{:S(2)}) %collective-permute-start.4) | collective-permute-done | bytes 73760 | tf_op jit(solution)/shard_map/ppermute | solution.py:299
  18.3 1.3 %collective-permute-start.2 = (f32[10,4,128]{2,1,0:T(4,128)S(1)}, f32[10,4,128]{2,1,0:T(4,128)S(1)}, u32[]{:S(2)}, u32[]{:S(2)}) collective-permute-start(f32[10,4,128]{2,1,0:T(4,128)S(1)} %get-tuple-element.15), channel_id=1, source_target_pairs={{1,0},{2,1},{3,2},{5,4},{6,5},{7,6},{9,8},{10,9},{11,10},{13,12},{... | collective-permute-start | bytes 61448 | tf_op jit(solution)/shard_map/ppermute | solution.py:340
  19.6 1.8 %collective-permute-done.5.rest_1_ = f32[144,128]{1,0:T(8,128)S(1)} collective-permute-done((f32[144,128]{1,0:T(8,128)S(1)}, f32[144,128]{1,0:T(8,128)S(1)}, u32[]{:S(2)}, u32[]{:S(2)}) %collective-permute-start.5) | collective-permute-done | bytes 73760 | tf_op jit(solution)/shard_map/ppermute | solution.py:299
  21.4 1.9 %collective-permute-done.6.rest_2_ = f32[144,128]{1,0:T(8,128)S(1)} collective-permute-done((f32[144,128]{1,0:T(8,128)S(1)}, f32[144,128]{1,0:T(8,128)S(1)}, u32[]{:S(2)}, u32[]{:S(2)}) %collective-permute-start.6) | collective-permute-done | bytes 73760 | tf_op jit(solution)/shard_map/ppermute | solution.py:299
  23.4 0.0 copy-start.2
  23.4 0.0 copy-start.3
  23.4 1.6 %collective-permute-start.7 = (f32[48,128]{1,0:T(8,128)S(1)}, f32[48,128]{1,0:T(8,128)S(1)}, u32[]{:S(2)}, u32[]{:S(2)}) collective-permute-start(f32[48,128]{1,0:T(8,128)S(1)} %reduce.1.rest_0_), channel_id=1, source_target_pairs={{0,1},{1,0},{2,3},{3,2},{4,5},{5,4},{6,7},{7,6},{8,9},{9,8},{10,11... | collective-permute-start | bytes 73736 | tf_op jit(solution)/shard_map/ppermute | solution.py:299
  24.9 1.5 %collective-permute-start.8 = (f32[48,128]{1,0:T(8,128)S(1)}, f32[48,128]{1,0:T(8,128)S(1)}, u32[]{:S(2)}, u32[]{:S(2)}) collective-permute-start(f32[48,128]{1,0:T(8,128)S(1)} %reduce.1.rest_0_), channel_id=1, source_target_pairs={{0,2},{1,3},{2,0},{3,1},{4,6},{5,7},{6,4},{7,5},{8,10},{9,11},{10,... | collective-permute-start | bytes 73736 | tf_op jit(solution)/shard_map/ppermute | solution.py:299
  26.5 0.5 %collective-permute-start.9 = (f32[48,128]{1,0:T(8,128)S(1)}, f32[48,128]{1,0:T(8,128)S(1)}, u32[]{:S(2)}, u32[]{:S(2)}) collective-permute-start(f32[48,128]{1,0:T(8,128)S(1)} %reduce.1.rest_0_), channel_id=1, source_target_pairs={{0,3},{1,2},{2,1},{3,0},{4,7},{5,6},{6,5},{7,4},{8,11},{9,10},{10,... | collective-permute-start | bytes 73736 | tf_op jit(solution)/shard_map/ppermute | solution.py:299
  26.9 8.7 %stencil.1.flow_in = f32[2,5,4,64,128]{4,3,2,1,0:T(8,128)S(1)} custom-call(f32[2,5,4,64,128]{4,3,2,1,0:T(8,128)S(1)} %copy-done.1, bf16[7,5,5,4,64,128]{5,4,3,2,1,0:T(8,128)(2,1)} %jac.3, f32[880,128]{1,0:T(8,128)S(1)} %collective-permute-done.got, f32[10,4,128]{2,1,0:T(4,128)S(1)} %collective-permute-done.1.lo, f32[10,4,128]{2,1,0:T(4,128)S(1)} %collective-permute-done.2.hi), custom_call_target="tpu_custom_call" | custom-call | flops 22937600 | bytes 14090240 | tf_op jit(solution)/shard_map/stencil/pallas_call | solution.py:354
  35.7 3.4 %couple.1 = (f32[2,5,4,64,128]{4,3,2,1,0:T(8,128)}, f32[12,2,256]{2,1,0:T(2,128)S(1)}) custom-call(f32[2,5,4,64,128]{4,3,2,1,0:T(8,128)S(1)} %stencil.1.flow_in, bf16[7,5,5,4,64,128]{5,4,3,2,1,0:T(8,128)(2,1)} %jac.3, f32[640,128]{1,0:T(8,128)S(1)} %collective-permute-done.3.far, f32[5,12,4,64]{3,2,1,0:T(4,128)S(1)} %copy-done.3, s32[4,64]{1,0:T(4,128)S(1)} %copy-done.6, ...), custom_call_target="tpu_custom_call" | custom-call | flops 20000000 | bytes 6000000 | tf_op jit(solution)/shard_map/couple/pallas_call | solution.py:386
  39.2 0.6 %last.1 = f32[12,2,256]{2,1,0:T(2,128)} custom-call(f32[12,2,256]{2,1,0:T(2,128)S(1)} %get-tuple-element.22.band, f32[48,128]{1,0:T(8,128)S(1)} %reduce.1.rest_0_, f32[48,128]{1,0:T(8,128)S(1)} %collective-permute-done.7.rest_1_, f32[48,128]{1,0:T(8,128)S(1)} %collective-permute-done.8.rest_2_, f32[48,128]{1,0:T(8,128)S(1)} %collective-permute-done.9.rest_3_), custom_call_target="tpu_custom_call" | custom-call | tf_op jit(solution)/shard_map/last/pallas_call | solution.py:404
  (18 shorter events, 0.1 us)
Async XLA Ops:
  0.6 1.3 %copy-start = (f32[2,5,4,64,128]{4,3,2,1,0:T(8,128)S(1)}, f32[2,5,4,64,128]{4,3,2,1,0:T(8,128)}, u32[]{:S(2)}) copy-start(f32[2,5,4,64,128]{4,3,2,1,0:T(8,128)} %flow.3) | copy-start | bytes 3932164
  1.9 0.9 %copy-start.4 = (f32[12,5,4,64]{3,2,1,0:T(4,128)S(1)}, f32[12,5,4,64]{3,2,1,0:T(4,128)}, u32[]{:S(2)}) copy-start(f32[12,5,4,64]{3,2,1,0:T(4,128)} %lmap.1) | copy-start | bytes 184324
  2.9 0.7 %copy-start.5 = (f32[2,12,256]{2,0,1:T(2,128)S(1)}, f32[2,12,256]{2,0,1:T(2,128)}, u32[]{:S(2)}) copy-start(f32[2,12,256]{2,0,1:T(2,128)} %param.10) | copy-start | bytes 73732
  3.6 0.7 %copy-start.6 = (s32[4,64]{1,0:T(4,128)S(1)}, s32[4,64]{1,0:T(4,128)}, u32[]{:S(2)}) copy-start(s32[4,64]{1,0:T(4,128)} %mask.3) | copy-start | bytes 3076
  4.3 0.7 %copy-start.7 = (s32[4,64]{1,0:T(4,128)S(1)}, s32[4,64]{1,0:T(4,128)}, u32[]{:S(2)}) copy-start(s32[4,64]{1,0:T(4,128)} %sta.3) | copy-start | bytes 3076
  5.0 22.0 %copy-start.1 = (f32[2,5,4,64,128]{4,3,2,1,0:T(8,128)S(1)}, f32[2,5,4,64,128]{4,3,2,1,0:T(8,128)}, u32[]{:S(2)}) copy-start(f32[2,5,4,64,128]{4,3,2,1,0:T(8,128)} %flow.3) | copy-start | bytes 3932164
  5.9 1.9 %collective-permute-start = (f32[880,128]{1,0:T(8,128)S(1)}, f32[880,128]{1,0:T(8,128)S(1)}, u32[]{:S(2)}, u32[]{:S(2)}) collective-permute-start(f32[880,128]{1,0:T(8,128)S(1)} %get-tuple-element.13.sent), channel_id=1, source_target_pairs={{0,4},{4,0},{8,12},{12,8},{16,20},{20,16},{24,28},{28,24},{1,5},{5... | collective-permute-start | bytes 1351688 | tf_op jit(solution)/shard_map/ppermute | solution.py:299
  6.4 29.3 %collective-permute-start.3 = (f32[640,128]{1,0:T(8,128)S(1)}, f32[640,128]{1,0:T(8,128)S(1)}, u32[]{:S(2)}, u32[]{:S(2)}) collective-permute-start(f32[640,128]{1,0:T(8,128)S(1)} %get-tuple-element.16), channel_id=1, source_target_pairs={{4,8},{8,4},{12,16},{16,12},{20,24},{24,20},{5,9},{9,5},{13,17},{1... | collective-permute-start | bytes 983048 | tf_op jit(solution)/shard_map/ppermute | solution.py:338
  7.9 10.4 %collective-permute-start.4 = (f32[144,128]{1,0:T(8,128)S(1)}, f32[144,128]{1,0:T(8,128)S(1)}, u32[]{:S(2)}, u32[]{:S(2)}) collective-permute-start(f32[144,128]{1,0:T(8,128)S(1)} %get-tuple-element.18), channel_id=1, source_target_pairs={{0,8},{4,12},{8,0},{12,4},{16,24},{20,28},{24,16},{28,20},{1,9},{5... | collective-permute-start | bytes 221192 | tf_op jit(solution)/shard_map/ppermute | solution.py:299
  11.0 10.4 %collective-permute-start.5 = (f32[144,128]{1,0:T(8,128)S(1)}, f32[144,128]{1,0:T(8,128)S(1)}, u32[]{:S(2)}, u32[]{:S(2)}) collective-permute-start(f32[144,128]{1,0:T(8,128)S(1)} %get-tuple-element.19), channel_id=1, source_target_pairs={{0,16},{4,20},{8,24},{12,28},{16,0},{20,4},{24,8},{28,12},{1,17},{... | collective-permute-start | bytes 221192 | tf_op jit(solution)/shard_map/ppermute | solution.py:299
  14.1 9.2 %collective-permute-start.6 = (f32[144,128]{1,0:T(8,128)S(1)}, f32[144,128]{1,0:T(8,128)S(1)}, u32[]{:S(2)}, u32[]{:S(2)}) collective-permute-start(f32[144,128]{1,0:T(8,128)S(1)} %get-tuple-element.20), channel_id=1, source_target_pairs={{0,24},{4,28},{8,16},{12,20},{16,8},{20,12},{24,0},{28,4},{1,25},{... | collective-permute-start | bytes 221192 | tf_op jit(solution)/shard_map/ppermute | solution.py:299
  14.1 12.3 %collective-permute-start.1 = (f32[10,4,128]{2,1,0:T(4,128)S(1)}, f32[10,4,128]{2,1,0:T(4,128)S(1)}, u32[]{:S(2)}, u32[]{:S(2)}) collective-permute-start(f32[10,4,128]{2,1,0:T(4,128)S(1)} %get-tuple-element.14), channel_id=1, source_target_pairs={{0,1},{1,2},{2,3},{4,5},{5,6},{6,7},{8,9},{9,10},{10,11},{12,13},{... | collective-permute-start | bytes 61448 | tf_op jit(solution)/shard_map/ppermute | solution.py:339
  18.3 8.6 %collective-permute-start.2 = (f32[10,4,128]{2,1,0:T(4,128)S(1)}, f32[10,4,128]{2,1,0:T(4,128)S(1)}, u32[]{:S(2)}, u32[]{:S(2)}) collective-permute-start(f32[10,4,128]{2,1,0:T(4,128)S(1)} %get-tuple-element.15), channel_id=1, source_target_pairs={{1,0},{2,1},{3,2},{5,4},{6,5},{7,6},{9,8},{10,9},{11,10},{13,12},{... | collective-permute-start | bytes 61448 | tf_op jit(solution)/shard_map/ppermute | solution.py:340
  23.4 12.3 %copy-start.2 = (f32[5,12,12,256]{3,2,1,0:T(8,128)S(1)}, f32[5,12,12,256]{3,2,1,0:T(8,128)}, u32[]{:S(2)}) copy-start(f32[5,12,12,256]{3,2,1,0:T(8,128)} %stiff.1) | copy-start | bytes 2211844
  23.4 12.3 %copy-start.3 = (f32[5,12,4,64]{3,2,1,0:T(4,128)S(1)}, f32[5,12,4,64]{3,2,1,0:T(4,128)}, u32[]{:S(2)}) copy-start(f32[5,12,4,64]{3,2,1,0:T(4,128)} %motion.1) | copy-start | bytes 184324
  23.4 15.7 %collective-permute-start.7 = (f32[48,128]{1,0:T(8,128)S(1)}, f32[48,128]{1,0:T(8,128)S(1)}, u32[]{:S(2)}, u32[]{:S(2)}) collective-permute-start(f32[48,128]{1,0:T(8,128)S(1)} %reduce.1.rest_0_), channel_id=1, source_target_pairs={{0,1},{1,0},{2,3},{3,2},{4,5},{5,4},{6,7},{7,6},{8,9},{9,8},{10,11... | collective-permute-start | bytes 73736 | tf_op jit(solution)/shard_map/ppermute | solution.py:299
  24.9 14.2 %collective-permute-start.8 = (f32[48,128]{1,0:T(8,128)S(1)}, f32[48,128]{1,0:T(8,128)S(1)}, u32[]{:S(2)}, u32[]{:S(2)}) collective-permute-start(f32[48,128]{1,0:T(8,128)S(1)} %reduce.1.rest_0_), channel_id=1, source_target_pairs={{0,2},{1,3},{2,0},{3,1},{4,6},{5,7},{6,4},{7,5},{8,10},{9,11},{10,... | collective-permute-start | bytes 73736 | tf_op jit(solution)/shard_map/ppermute | solution.py:299
  26.5 12.7 %collective-permute-start.9 = (f32[48,128]{1,0:T(8,128)S(1)}, f32[48,128]{1,0:T(8,128)S(1)}, u32[]{:S(2)}, u32[]{:S(2)}) collective-permute-start(f32[48,128]{1,0:T(8,128)S(1)} %reduce.1.rest_0_), channel_id=1, source_target_pairs={{0,3},{1,2},{2,1},{3,0},{4,7},{5,6},{6,5},{7,4},{8,11},{9,10},{10,... | collective-permute-start | bytes 73736 | tf_op jit(solution)/shard_map/ppermute | solution.py:299
where the time goes:
time: 40.2 us; the launch traced here: 39.8 us
  starting transfers between devices  15.7 us (39%)
  Pallas kernels  13.7 us (34%)
  waiting for transfers between devices  5.28 us (13%)
  local copies, waits for them, and re-layouts  4.33 us (11%)
  between operations  0.76 us (2%)
    ppermute x7, starting transfers between devices, swap(): lax.ppermute(x, axis, [(i, i ^ m) for i in range(lax.axis_size(axis))])  10.3 us
    pallas_call x1, Pallas kernels, on_device(): pl.pallas_call(stencil_kernel, grid=(srows,), out_shape=jax.ShapeDtypeStr...  8.73 us
    ppermute x7, waiting for transfers between devices, swap(): lax.ppermute(x, axis, [(i, i ^ m) for i in range(lax.axis_size(axis))])  5.28 us
    unnamed x16, local copies, waits for them, and re-layouts  4.33 us
    pallas_call x1, Pallas kernels, on_device(): pl.pallas_call(functools.partial(couple_kernel, span), out_shape=(jax.Sha...  3.41 us
    ppermute x1, starting transfers between devices, on_device(): lo = lax.ppermute(up, 'chord', [(i, i + 1) for i in range(chord - 1)])  3.39 us
    ppermute x1, starting transfers between devices, on_device(): hi = lax.ppermute(down, 'chord', [(i + 1, i) for i in range(chord - 1)])  1.28 us
    pallas_call x1, Pallas kernels, on_device(): pl.pallas_call(functools.partial(pre_kernel, span), out_shape=(shape(halo...  0.93 us
  transfers between devices with their start and end apart: 10, of which 4 were waited for; matrix products, arithmetic and copies ran while one was open for 0% of the time, Pallas kernels for 31%

commit v1 on v0

v1 whole, which is shorter than its diff:
```python
import functools

import jax
import jax.numpy as jnp
from jax import lax
from jax.experimental import pallas as pl
from jax.experimental.pallas import tpu as pltpu
from jax.sharding import PartitionSpec as P

F32 = jnp.float32
BF16 = jnp.bfloat16
LANES = 128
VMEM = pl.BlockSpec(memory_space=pltpu.VMEM)
LIMIT = 16 * 1024 * 1024
FIRST = 20000000000


def params():
    return pltpu.CompilerParams(vmem_limit_bytes=LIMIT)


def halves(x):
    hi = x.astype(BF16).astype(F32)
    return jnp.concatenate([hi, x - hi], axis=0).astype(BF16)


def lane_row(x, width):
    return jnp.concatenate([x[r : r + 1, :width] for r in range(x.shape[0])], axis=1)


def table(stations, first, count):
    rows = lax.broadcasted_iota(jnp.int32, (count, stations.shape[1]), 0) + first
    return (rows == stations).astype(F32).astype(BF16)


def put_slabs(ref, base, rows):
    n = rows.shape[0]
    for h in range(rows.shape[1] // LANES):
        ref[base + h * n : base + (h + 1) * n] = rows[:, h * LANES : (h + 1) * LANES]


def get_slabs(ref, base, n, k):
    return jnp.concatenate([ref[base + h * n : base + (h + 1) * n] for h in range(k)], axis=1)


def relative(sta, me, sta_dev, ccols):
    return lane_row(sta[...] ^ (me * sta_dev), ccols)


def face_kernel(flow, near, far, beside, across, surf):
    nvec, nvar, srows, ccols, _ = flow.shape
    odd = lax.axis_index("span") % 2 == 1
    near_row = jnp.where(odd, 0, srows - 1)
    far_row = srows - 1 - near_row
    codd = lax.axis_index("chord") % 2 == 1
    near_col = jnp.where(codd, 0, 1)
    lane = lax.broadcasted_iota(jnp.int32, (ccols, LANES), 1)
    packed = jnp.zeros((ccols, LANES), F32)
    for v in range(nvec):
        for b in range(nvar):
            q = v * nvar + b
            near[q * ccols : (q + 1) * ccols] = flow[v, b, near_row]
            far[q * ccols : (q + 1) * ccols] = flow[v, b, far_row]
            low, high = flow[v, b, :, 0, :], flow[v, b, :, ccols - 1, :]
            beside[q] = jnp.where(near_col == 0, low, high)
            across[q] = jnp.where(near_col == 0, high, low)
            for r in range(srows):
                at = q * 8 + r
                x = flow[v, b, r]
                if at:
                    x = pltpu.roll(x, at, 1)
                packed = jnp.where(lane == at, x, packed)
    surf[...] = packed.T


def pre_kernel(span, surf_in, lmap, mask, sta, beam, p1, kept, rel, maskf_out, wall):
    nvar = lmap.shape[1]
    srows, ccols = mask.shape
    ndof, nvec, sta_dev = beam.shape
    k = sta_dev // LANES
    rows = nvec * ndof
    me = lax.axis_index("span")
    surf = surf_in[...]
    maskf = mask[...].astype(F32)
    maskf_out[...] = maskf
    for v in range(nvec):
        near = [surf[(v * nvar + a) * 8 : (v * nvar + a) * 8 + srows] * maskf for a in range(nvar)]
        for j in range(ndof):
            total = lmap[j, 0] * near[0]
            for a in range(1, nvar):
                total = total + lmap[j, a] * near[a]
            wall[v * ndof + j] = total
    walls = jnp.concatenate([wall[:, r, :] for r in range(srows)], axis=1)
    parts = halves(walls)
    stations = relative(sta, me, sta_dev, ccols)
    rel[...] = stations
    for p in range(span):
        both = lax.dot_general(
            parts,
            table(stations, p * sta_dev, sta_dev),
            (((1,), (1,)), ((), ())),
            preferred_element_type=F32,
        )
        put_slabs(p1 if p % 2 else kept, (p // 2) * rows * k, both[:rows] + both[rows:])
    base = (span // 2) * rows * k
    for v in range(nvec):
        for j in range(ndof):
            for h in range(k):
                at = base + h * rows + v * ndof + j
                p1[at : at + 1] = beam[j, v : v + 1, h * LANES : (h + 1) * LANES]


def combine_kernel(slab, sent, got, kept, own, *out):
    groups = len(out) + 1
    base = groups * slab
    own[...] = kept[:slab] + got[:slab]
    for q in range(1, groups):
        o = out[q - 1]
        o[:slab] = kept[q * slab : (q + 1) * slab] + got[q * slab : (q + 1) * slab]
        o[slab : 2 * slab] = sent[base : base + slab]
        o[2 * slab :] = got[base : base + slab]


def stencil_kernel(chord, flow, jac, got, beside, across, out, near):
    nvec, nvar, srows, ccols, _ = flow.shape
    me = lax.axis_index("span")
    odd = me % 2
    row = lax.broadcasted_iota(jnp.int32, (ccols, LANES), 0)
    lane = lax.broadcasted_iota(jnp.int32, (ccols, LANES), 1)
    low_on = jnp.where(odd == 1, 1.0, 0.0).astype(F32)
    high_on = 1.0 - low_on
    column = lax.axis_index("chord")
    codd = column % 2
    inner = jnp.where((column > 0) & (column < chord - 1), 1.0, 0.0).astype(F32)
    tile = 16

    def one_row(r, carry):
        for v in range(nvec):
            for b in range(nvar):
                q = v * nvar + b
                x = flow[v, b, r]
                left, right = pltpu.roll(x, 1, 0), pltpu.roll(x, ccols - 1, 0)
                one, two = beside[q, pl.ds(r, 1)], across[q, pl.ds(r, 1)] * inner
                near[0, q] = jnp.where(row == 0, jnp.where(codd == 1, one, two), left)
                near[1, q] = jnp.where(row == ccols - 1, jnp.where(codd == 1, two, one), right)
                near[2, q] = jnp.where(lane == 0, 0.0, pltpu.roll(x, 1, 1))
                near[3, q] = jnp.where(lane == LANES - 1, 0.0, pltpu.roll(x, LANES - 1, 1))
        first, last = r == 0, r == srows - 1
        below = jnp.where(first, 0, r - 1)
        above = jnp.where(last, srows - 1, r + 1)

        def one_tile(t, carry):
            c = pl.multiple_of(t * tile, tile)
            here = pl.ds(c, tile)
            acc = [[jnp.zeros((tile, LANES), F32) for _ in range(nvar)] for _ in range(nvec)]
            for e in range(7):
                for b in range(nvar):
                    xs = []
                    for v in range(nvec):
                        q = v * nvar + b
                        if e == 0:
                            x = flow[v, b, r, here]
                        elif e == 1:
                            h = got[pl.ds(q * ccols + c, tile)] * low_on
                            x = jnp.where(first, h, flow[v, b, below, here])
                        elif e == 2:
                            h = got[pl.ds(q * ccols + c, tile)] * high_on
                            x = jnp.where(last, h, flow[v, b, above, here])
                        else:
                            x = near[e - 3, q, here]
                        xs.append(x)
                    for a in range(nvar):
                        m = jac[e, a, b, r, here].astype(F32)
                        for v in range(nvec):
                            acc[v][a] = acc[v][a] + m * xs[v]
            for v in range(nvec):
                for a in range(nvar):
                    out[v, a, r, here] = acc[v][a]
            return carry

        return lax.fori_loop(0, ccols // tile, one_tile, carry)

    lax.fori_loop(0, srows, one_row, 0)


def couple_kernel(
    span, flow_in, jac, far, motion, mask, rel, stiff, sent, got, *rest
):
    groups = span // 2
    zs = rest[: groups - 1]
    flow, band, gath, lk = rest[groups - 1 :]
    nvec, nvar, srows, ccols, _ = flow_in.shape
    _, ndof, _, sta_dev = stiff.shape
    k = sta_dev // LANES
    rows = nvec * ndof
    slab = rows * k
    me = lax.axis_index("span")
    odd = me % 2
    e = 1 + odd
    inner = jnp.where((me > 0) & (me < span - 1), 1.0, 0.0).astype(F32)
    r_far = jnp.where(odd == 1, srows - 1, 0)
    base = groups * slab
    gath[0] = get_slabs(sent, base, rows, k)
    gath[1] = get_slabs(got, base, rows, k)
    for q in range(1, groups):
        gath[2 * q] = get_slabs(zs[q - 1], slab, rows, k)
        gath[2 * q + 1] = get_slabs(zs[q - 1], 2 * slab, rows, k)
    stations = rel[...]
    both = jnp.zeros((2 * rows, srows * ccols), F32)
    for p in range(span):
        both = both + jnp.dot(
            halves(gath[p]), table(stations, p * sta_dev, sta_dev), preferred_element_type=F32
        )
    looked = both[:rows] + both[rows:]
    for r in range(srows):
        lk[:, r, :] = looked[:, r * ccols : (r + 1) * ccols]
    maskf = mask[...]
    tiles = []
    for v in range(nvec):
        for a in range(nvar):
            total = motion[a, 0] * lk[v * ndof]
            for j in range(1, ndof):
                total = total + motion[a, j] * lk[v * ndof + j]
            total = total * maskf
            tiles.append(jnp.concatenate([total, jnp.zeros((8 - srows, ccols), F32)], axis=0))
    tiles.append(jnp.zeros((LANES - 8 * len(tiles), ccols), F32))
    packed = jnp.concatenate(tiles, axis=0).T
    lane = lax.broadcasted_iota(jnp.int32, (ccols, LANES), 1)
    for v in range(nvec):
        for a in range(nvar):
            for r in range(srows):
                at = (v * nvar + a) * 8 + r
                x = packed if at == 0 else pltpu.roll(packed, LANES - at, 1)
                flow[v, a, r] = flow_in[v, a, r] + jnp.where(lane == 0, x, 0.0)
    own = gath[0]
    before = gath[jnp.where(me > 0, me ^ (me - 1), 0)]
    after = gath[jnp.where(me < span - 1, me ^ (me + 1), 0)]
    pos = lax.broadcasted_iota(jnp.int32, (rows, sta_dev), 1)
    place = pos + me * sta_dev
    stations_all = span * sta_dev
    blade_len = stations_all // 4

    def blade(t):
        n = jnp.zeros(t.shape, jnp.int32)
        for m in range(1, 5):
            n = n + (t + sta_dev // 2 >= m * blade_len).astype(jnp.int32)
        return n

    home = blade(place)
    shifted = []
    for d in range(5):
        s = d - 2
        other = place + s
        x = own if s == 0 else pltpu.roll(own, (-s) % sta_dev, 1)
        if s < 0:
            x = jnp.where(pos < -s, pltpu.roll(before, -s, 1), x)
        if s > 0:
            x = jnp.where(pos >= sta_dev - s, pltpu.roll(after, sta_dev - s, 1), x)
        good = (blade(other) == home) & (other >= 0) & (other < stations_all)
        x = jnp.where(good, x, 0.0)
        shifted.append([x[v * ndof : (v + 1) * ndof] for v in range(nvec)])
    for i in range(ndof):
        for v in range(nvec):
            total = stiff[0, i] * shifted[0][v]
            for d in range(1, 5):
                total = total + stiff[d, i] * shifted[d][v]
            band[i, v : v + 1, :] = jnp.sum(total, axis=0, keepdims=True)
    tile = 16

    def body(t, carry):
        c = pl.multiple_of(t * tile, tile)
        here = pl.ds(c, tile)
        acc = [[flow[v, a, r_far, here] for a in range(nvar)] for v in range(nvec)]
        for b in range(nvar):
            xs = [far[pl.ds((v * nvar + b) * ccols + c, tile)] * inner for v in range(nvec)]
            for a in range(nvar):
                m = jac[e, a, b, r_far, here].astype(F32)
                for v in range(nvec):
                    acc[v][a] = acc[v][a] + m * xs[v]
        for v in range(nvec):
            for a in range(nvar):
                flow[v, a, r_far, here] = acc[v][a]
        return carry

    lax.fori_loop(0, ccols // tile, body, 0)


def last_kernel(band, *rest):
    parts, out = rest[:-1], rest[-1]
    ndof, nvec, sta_dev = band.shape
    rows = ndof * nvec
    total = parts[0][...]
    for p in parts[1:]:
        total = total + p[...]
    for v in range(nvec):
        for j in range(ndof):
            for h in range(sta_dev // LANES):
                at = h * rows + v * ndof + j
                cols = slice(h * LANES, (h + 1) * LANES)
                out[j, v : v + 1, cols] = band[j, v : v + 1, cols] - total[at : at + 1]


def reduce_kernel(_, own, *rest):
    parts, out = rest[:-1], rest[-1]
    total = own[...]
    for p in parts:
        total = total + p[: total.shape[0]]
    out[...] = total


def swap(x, axis, m):
    return lax.ppermute(x, axis, [(i, i ^ m) for i in range(lax.axis_size(axis))])


def others(span, chord, along_span):
    pairs = []
    for i in range(span):
        for c in range(chord):
            at, size = (i, span) if along_span else (c, chord)
            if 0 < at < size - 1:
                to = at + 1 if at % 2 else at - 1
                to = (to, c) if along_span else (i, to)
            else:
                to = (i, c ^ 1) if along_span else (i ^ 1, c)
            pairs.append((i * chord + c, to[0] * chord + to[1]))
    return pairs


def on_device(
    flow_state, jacobians, beam_state, stiffness, motion_map, load_map, surface_mask, station_of
):
    nvec, nvar, srows, ccols, ncell = flow_state.shape
    ndof, sta_dev = beam_state.shape[1:]
    span, chord = lax.axis_size("span"), lax.axis_size("chord")
    groups = span // 2
    k = sta_dev // LANES
    rows = nvec * ndof
    slab = rows * k
    halo = nvec * nvar * ccols
    nq = nvec * nvar
    beam = jnp.transpose(beam_state, (1, 0, 2))

    def shape(*s):
        return jax.ShapeDtypeStruct(s, F32)

    near, far, beside, across, surf = pl.pallas_call(
        face_kernel,
        out_shape=(
            shape(halo, LANES),
            shape(halo, LANES),
            shape(nq, srows, LANES),
            shape(nq, srows, LANES),
            shape(LANES, ccols),
        ),
        in_specs=[VMEM],
        out_specs=(VMEM,) * 5,
        compiler_params=params(),
        cost_estimate=pl.CostEstimate(flops=FIRST, bytes_accessed=2000000, transcendentals=0),
        name="faces",
    )(flow_state)
    far_got = lax.ppermute(far, ("span", "chord"), others(span, chord, True))
    beside_got = swap(beside, "chord", 1)
    across_got = lax.ppermute(across, ("span", "chord"), others(span, chord, False))
    near_got = swap(near, "span", 1)

    p1, kept, rel, maskf = pl.pallas_call(
        functools.partial(pre_kernel, span),
        out_shape=(
            shape((groups + 1) * slab, LANES),
            shape(groups * slab, LANES),
            jax.ShapeDtypeStruct((1, srows * ccols), jnp.int32),
            shape(srows, ccols),
        ),
        in_specs=[VMEM] * 5,
        out_specs=(VMEM,) * 4,
        scratch_shapes=[pltpu.VMEM((rows, srows, ccols), F32)],
        compiler_params=params(),
        cost_estimate=pl.CostEstimate(flops=FIRST, bytes_accessed=1000000, transcendentals=0),
        name="pre",
    )(surf, load_map, surface_mask, station_of, beam)
    p1_got = swap(p1, "span", 1)

    own, *zs = pl.pallas_call(
        functools.partial(combine_kernel, slab),
        out_shape=(shape(slab, LANES),) + (shape(3 * slab, LANES),) * (groups - 1),
        in_specs=[VMEM] * 3,
        out_specs=(VMEM,) * groups,
        compiler_params=params(),
        name="combine",
    )(p1, p1_got, kept)
    z_got = [swap(zs[q - 1], "span", 2 * q) for q in range(1, groups)]

    flow1 = pl.pallas_call(
        functools.partial(stencil_kernel, chord),
        out_shape=jax.ShapeDtypeStruct(flow_state.shape, F32),
        in_specs=[VMEM] * 5,
        out_specs=VMEM,
        scratch_shapes=[pltpu.VMEM((4, nq, ccols, LANES), F32)],
        compiler_params=params(),
        cost_estimate=pl.CostEstimate(
            flops=4 * 7 * nvar * nvar * srows * ccols * ncell,
            bytes_accessed=2 * jacobians.size + 8 * flow_state.size,
            transcendentals=0,
        ),
        name="stencil",
    )(flow_state, jacobians, near_got, beside_got, across_got)

    loads = pl.pallas_call(
        reduce_kernel,
        out_shape=shape(slab, LANES),
        in_specs=[pl.BlockSpec(memory_space=pl.ANY)] + [VMEM] * groups,
        out_specs=VMEM,
        compiler_params=params(),
        name="reduce",
    )(flow1, own, *z_got)
    chord_got = [swap(loads, "chord", m) for m in range(1, chord)]

    flow_image, band = pl.pallas_call(
        functools.partial(couple_kernel, span),
        out_shape=(jax.ShapeDtypeStruct(flow_state.shape, F32), shape(ndof, nvec, sta_dev)),
        in_specs=[VMEM] * (9 + groups - 1),
        out_specs=(VMEM, VMEM),
        scratch_shapes=[
            pltpu.VMEM((span, rows, sta_dev), F32),
            pltpu.VMEM((rows, srows, ccols), F32),
        ],
        compiler_params=params(),
        cost_estimate=pl.CostEstimate(flops=20000000, bytes_accessed=6000000, transcendentals=0),
        name="couple",
    )(
        flow1, jacobians, far_got, motion_map, maskf, rel, stiffness, p1, p1_got, *z_got
    )

    out = pl.pallas_call(
        last_kernel,
        out_shape=shape(ndof, nvec, sta_dev),
        in_specs=[VMEM] * (chord + 1),
        out_specs=VMEM,
        compiler_params=params(),
        name="last",
    )(band, loads, *chord_got)
    return flow_image, jnp.transpose(out, (1, 0, 2))


def solution(mesh):
    in_specs = (
        P(None, None, "span", "chord", None),
        P(None, None, None, "span", "chord", None),
        P(None, None, "span"),
        P(None, None, None, "span"),
        P(None, None, "span", "chord"),
        P(None, None, "span", "chord"),
        P("span", "chord"),
        P("span", "chord"),
    )
    out_specs = (P(None, None, "span", "chord", None), P(None, None, "span"))
    return jax.shard_map(
        on_device, mesh=mesh, in_specs=in_specs, out_specs=out_specs, check_vma=False
    )
```

time: 40.2 us -> 29.7 us (0.74)
  Pallas kernels: 13.7 us -> 10.5 us
  local copies, waits for them, and re-layouts: 4.33 us -> 1.36 us
  waiting for transfers between devices: 5.28 us -> 2.98 us
  starting transfers between devices: 15.7 us -> 13.9 us
    unnamed x16 -> x22, local copies, waits for them, and re-layouts: 4.33 us -> 1.36 us
    ppermute x3 -> x2, starting transfers between devices: 5.34 us -> 2.57 us  [the longest x1 2.56 us: on_device(): far_got = lax.ppermute(far, ('span', 'chord'), others(span, chord, True))]
    ppermute x7 -> x9, waiting for transfers between devices: 5.28 us -> 2.97 us  [swap(): lax.ppermute(x, axis, [(i, i ^ m) for i in range(lax.axis_size(axis))])]
    pallas_call x4 -> x5, Pallas kernels: 9.69 us -> 7.58 us  [the longest x1 6.55 us: on_device(): pl.pallas_call(functools.partial(stencil_kernel, chord), out_shape=jax.Sh...]
    pallas_call x1, Pallas kernels: 3.41 us -> 2.32 us  [on_device(): pl.pallas_call(functools.partial(couple_kernel, span), out_shape=(jax.Sha...]
    ppermute x7 -> x9, starting transfers between devices: 10.3 us -> 11.3 us  [swap(): lax.ppermute(x, axis, [(i, i ^ m) for i in range(lax.axis_size(axis))])]
  transfers between devices with their start and end apart: 10 -> 11, of which waited for: 4 -> 2; matrix products, arithmetic and copies ran while one was open for 0% -> 0% of each run, Pallas kernels for 31% -> 32%
where the time goes in v1:
time: 29.7 us; the launch traced here: 29.6 us
  starting transfers between devices  13.9 us (47%)
  Pallas kernels  10.5 us (35%)
  waiting for transfers between devices  2.98 us (10%)
  local copies, waits for them, and re-layouts  1.36 us (5%)
  between operations  0.8 us (3%)
    ppermute x9, starting transfers between devices, swap(): lax.ppermute(x, axis, [(i, i ^ m) for i in range(lax.axis_size(axis))])  11.3 us
    pallas_call x1, Pallas kernels, on_device(): pl.pallas_call(functools.partial(stencil_kernel, chord), out_shape=jax.Sh...  6.55 us
    ppermute x9, waiting for transfers between devices, swap(): lax.ppermute(x, axis, [(i, i ^ m) for i in range(lax.axis_size(axis))])  2.97 us
    ppermute x1, starting transfers between devices, on_device(): far_got = lax.ppermute(far, ('span', 'chord'), others(span, chord, True))  2.56 us
    pallas_call x1, Pallas kernels, on_device(): pl.pallas_call(functools.partial(couple_kernel, span), out_shape=(jax.Sha...  2.32 us
    unnamed x22, local copies, waits for them, and re-layouts  1.36 us
    pallas_call x1, Pallas kernels, on_device(): pl.pallas_call(last_kernel, out_shape=shape(ndof, nvec, sta_dev), in_spec...  0.63 us
  transfers between devices with their start and end apart: 11, of which 2 were waited for; matrix products, arithmetic and copies ran while one was open for 0% of the time, Pallas kernels for 32%

profile of v1, /device:TPU:0, one launch (start us, length us, event | category | flops | bytes accessed | tf_op | source)
XLA Modules:
  0.0 29.6 jit_solution(15527293882280992213)
XLA Ops:
  0.6 0.0 copy-start
  0.6 1.3 %copy-done = f32[2,5,4,64,128]{4,3,2,1,0:T(8,128)S(1)} copy-done((f32[2,5,4,64,128]{4,3,2,1,0:T(8,128)S(1)}, f32[2,5,4,64,128]{4,3,2,1,0:T(8,128)}, u32[]{:S(2)}) %copy-start) | copy-done | bytes 1310744
  2.0 0.5 %faces.1 = (f32[640,128]{1,0:T(8,128)S(1)}, f32[640,128]{1,0:T(8,128)S(1)}, f32[10,4,128]{2,1,0:T(4,128)S(1)}, f32[10,4,128]{2,1,0:T(4,128)S(1)}, f32[128,64]{1,0:T(8,128)S(1)}) custom-call(f32[2,5,4,64,128]{4,3,2,1,0:T(8,128)S(1)} %copy-done), custom_call_target="tpu_custom_call" | custom-call | flops 20000000000 | bytes 2000000 | tf_op jit(solution)/shard_map/faces/pallas_call | solution.py:346
  2.4 0.5 %collective-permute-start = (f32[640,128]{1,0:T(8,128)S(1)}, f32[640,128]{1,0:T(8,128)S(1)}, u32[]{:S(2)}, u32[]{:S(2)}) collective-permute-start(f32[640,128]{1,0:T(8,128)S(1)} %get-tuple-element.17), channel_id=1, source_target_pairs={{0,4},{4,0},{8,12},{12,8},{16,20},{20,16},{24,28},{28,24},{1,5},{5... | collective-permute-start | bytes 983048 | tf_op jit(solution)/shard_map/ppermute | solution.py:312
  3.0 2.6 %collective-permute-start.3 = (f32[640,128]{1,0:T(8,128)S(1)}, f32[640,128]{1,0:T(8,128)S(1)}, u32[]{:S(2)}, u32[]{:S(2)}) collective-permute-start(f32[640,128]{1,0:T(8,128)S(1)} %get-tuple-element.20), channel_id=1, source_target_pairs={{0,1},{1,0},{2,3},{3,2},{4,8},{5,9},{6,10},{7,11},{8,4},{9,5},{10,... | collective-permute-start | bytes 983048 | tf_op jit(solution)/shard_map/ppermute | solution.py:361
  5.6 0.0 slice-start.2
  5.6 0.0 copy-start.1
  5.6 0.5 %pre.1 = (f32[240,128]{1,0:T(8,128)S(1)}, f32[192,128]{1,0:T(8,128)S(1)}, s32[1,256]{1,0:T(1,128)S(1)}, f32[4,64]{1,0:T(4,128)S(1)}) custom-call(f32[128,64]{1,0:T(8,128)S(1)} %get-tuple-element.21.surf_in, f32[12,5,4,64]{3,2,1,0:T(4,128)S(1)} %copy-done.4, s32[4,64]{1,0:T(4,128)S(1)} %copy-done.6, s32[4,64]{1,0:T(4,128)S(1)} %copy-done.7, ...), custom_call_target="tpu_custom_call" | custom-call | flops 20000000000 | bytes 1000000 | tf_op jit(solution)/shard_map/pre/pallas_call | solution.py:366
  6.1 0.3 collective-permute-start.4
  6.4 1.5 %collective-permute-start.1 = (f32[10,4,128]{2,1,0:T(4,128)S(1)}, f32[10,4,128]{2,1,0:T(4,128)S(1)}, u32[]{:S(2)}, u32[]{:S(2)}) collective-permute-start(f32[10,4,128]{2,1,0:T(4,128)S(1)} %get-tuple-element.18), channel_id=1, source_target_pairs={{0,1},{1,0},{2,3},{3,2},{4,5},{5,4},{6,7},{7,6},{8,9},{9,8},{10,11... | collective-permute-start | bytes 61448 | tf_op jit(solution)/shard_map/ppermute | solution.py:312
  7.9 1.6 %collective-permute-start.5 = (f32[144,128]{1,0:T(8,128)S(1)}, f32[144,128]{1,0:T(8,128)S(1)}, u32[]{:S(2)}, u32[]{:S(2)}) collective-permute-start(f32[144,128]{1,0:T(8,128)S(1)} %get-tuple-element.26), channel_id=1, source_target_pairs={{0,8},{4,12},{8,0},{12,4},{16,24},{20,28},{24,16},{28,20},{1,9},{5... | collective-permute-start | bytes 221192 | tf_op jit(solution)/shard_map/ppermute | solution.py:312
  9.5 1.5 %collective-permute-done.1.beside = f32[10,4,128]{2,1,0:T(4,128)S(1)} collective-permute-done((f32[10,4,128]{2,1,0:T(4,128)S(1)}, f32[10,4,128]{2,1,0:T(4,128)S(1)}, u32[]{:S(2)}, u32[]{:S(2)}) %collective-permute-start.1) | collective-permute-done | bytes 20512 | tf_op jit(solution)/shard_map/ppermute | solution.py:312
  11.0 1.7 %collective-permute-start.6 = (f32[144,128]{1,0:T(8,128)S(1)}, f32[144,128]{1,0:T(8,128)S(1)}, u32[]{:S(2)}, u32[]{:S(2)}) collective-permute-start(f32[144,128]{1,0:T(8,128)S(1)} %get-tuple-element.27), channel_id=1, source_target_pairs={{0,16},{4,20},{8,24},{12,28},{16,0},{20,4},{24,8},{28,12},{1,17},{... | collective-permute-start | bytes 221192 | tf_op jit(solution)/shard_map/ppermute | solution.py:312
  12.7 0.0 collective-permute-done.2.across
  12.7 1.3 %collective-permute-start.7 = (f32[144,128]{1,0:T(8,128)S(1)}, f32[144,128]{1,0:T(8,128)S(1)}, u32[]{:S(2)}, u32[]{:S(2)}) collective-permute-start(f32[144,128]{1,0:T(8,128)S(1)} %get-tuple-element.28), channel_id=1, source_target_pairs={{0,24},{4,28},{8,16},{12,20},{16,8},{20,12},{24,0},{28,4},{1,25},{... | collective-permute-start | bytes 221192 | tf_op jit(solution)/shard_map/ppermute | solution.py:312
  14.1 6.5 %stencil.1.flow_in._ = f32[2,5,4,64,128]{4,3,2,1,0:T(8,128)S(1)} custom-call(f32[2,5,4,64,128]{4,3,2,1,0:T(8,128)S(1)} %copy-done.1, bf16[7,5,5,4,64,128]{5,4,3,2,1,0:T(8,128)(2,1)S(1)} %bitcast.3, f32[640,128]{1,0:T(8,128)S(1)} %collective-permute-done.got, f32[10,4,128]{2,1,0:T(4,128)S(1)} %collective-permute-done.1.beside, ...), custom_call_target="tpu_custom_call" | custom-call | flops 22937600 | bytes 14090240 | tf_op jit(solution)/shard_map/stencil/pallas_call | solution.py:393
  20.7 0.0 copy-start.2
  20.7 0.0 copy-start.3
  20.7 0.0 collective-permute-done.6.rest_1_
  20.8 2.5 %collective-permute-start.10 = (f32[48,128]{1,0:T(8,128)S(1)}, f32[48,128]{1,0:T(8,128)S(1)}, u32[]{:S(2)}, u32[]{:S(2)}) collective-permute-start(f32[48,128]{1,0:T(8,128)S(1)} %reduce.1.rest_0_), channel_id=1, source_target_pairs={{0,3},{1,2},{2,1},{3,0},{4,7},{5,6},{6,5},{7,4},{8,11},{9,10},{10,... | collective-permute-start | bytes 73736 | tf_op jit(solution)/shard_map/ppermute | solution.py:312
  23.3 1.8 %collective-permute-start.9 = (f32[48,128]{1,0:T(8,128)S(1)}, f32[48,128]{1,0:T(8,128)S(1)}, u32[]{:S(2)}, u32[]{:S(2)}) collective-permute-start(f32[48,128]{1,0:T(8,128)S(1)} %reduce.1.rest_0_), channel_id=1, source_target_pairs={{0,2},{1,3},{2,0},{3,1},{4,6},{5,7},{6,4},{7,5},{8,10},{9,11},{10,... | collective-permute-start | bytes 73736 | tf_op jit(solution)/shard_map/ppermute | solution.py:312
  25.1 2.3 %couple.1 = (f32[2,5,4,64,128]{4,3,2,1,0:T(8,128)}, f32[12,2,256]{2,1,0:T(2,128)S(1)}) custom-call(f32[2,5,4,64,128]{4,3,2,1,0:T(8,128)S(1)} %stencil.1.flow_in._, bf16[7,5,5,4,64,128]{5,4,3,2,1,0:T(8,128)(2,1)S(1)} %bitcast.3, f32[640,128]{1,0:T(8,128)S(1)} %collective-permute-done.3.far, f32[5,12,4,64]{3,2,1,0:T(4,128)S(1)} %copy-done.3, ...), custom_call_target="tpu_custom_call" | custom-call | flops 20000000 | bytes 6000000 | tf_op jit(solution)/shard_map/couple/pallas_call | solution.py:418
  27.5 1.5 %collective-permute-done.8.rest_1_ = f32[48,128]{1,0:T(8,128)S(1)} collective-permute-done((f32[48,128]{1,0:T(8,128)S(1)}, f32[48,128]{1,0:T(8,128)S(1)}, u32[]{:S(2)}, u32[]{:S(2)}) %collective-permute-start.8) | collective-permute-done | bytes 24608 | tf_op jit(solution)/shard_map/ppermute | solution.py:312
  28.9 0.6 %last.1 = f32[12,2,256]{2,1,0:T(2,128)} custom-call(f32[12,2,256]{2,1,0:T(2,128)S(1)} %get-tuple-element.30.band, f32[48,128]{1,0:T(8,128)S(1)} %reduce.1.rest_0_, f32[48,128]{1,0:T(8,128)S(1)} %collective-permute-done.8.rest_1_, f32[48,128]{1,0:T(8,128)S(1)} %collective-permute-done.9.rest_2_, f32[48,128]{1,0:T(8,128)S(1)} %collective-permute-done.10.rest_3_), custom_call_target="tpu_custom_call" | custom-call | tf_op jit(solution)/shard_map/last/pallas_call | solution.py:434
  (28 shorter events, 0.1 us)
Async XLA Ops:
  0.6 1.3 %copy-start = (f32[2,5,4,64,128]{4,3,2,1,0:T(8,128)S(1)}, f32[2,5,4,64,128]{4,3,2,1,0:T(8,128)}, u32[]{:S(2)}) copy-start(f32[2,5,4,64,128]{4,3,2,1,0:T(8,128)} %flow.3) | copy-start | bytes 3932164
  2.0 3.6 %copy-start.4 = (f32[12,5,4,64]{3,2,1,0:T(4,128)S(1)}, f32[12,5,4,64]{3,2,1,0:T(4,128)}, u32[]{:S(2)}) copy-start(f32[12,5,4,64]{3,2,1,0:T(4,128)} %lmap.1) | copy-start | bytes 184324
  2.0 3.6 %copy-start.5 = (f32[2,12,256]{2,0,1:T(2,128)S(1)}, f32[2,12,256]{2,0,1:T(2,128)}, u32[]{:S(2)}) copy-start(f32[2,12,256]{2,0,1:T(2,128)} %param.10) | copy-start | bytes 73732
  2.0 3.6 %copy-start.6 = (s32[4,64]{1,0:T(4,128)S(1)}, s32[4,64]{1,0:T(4,128)}, u32[]{:S(2)}) copy-start(s32[4,64]{1,0:T(4,128)} %mask.1) | copy-start | bytes 3076
  2.0 3.6 %copy-start.7 = (s32[4,64]{1,0:T(4,128)S(1)}, s32[4,64]{1,0:T(4,128)}, u32[]{:S(2)}) copy-start(s32[4,64]{1,0:T(4,128)} %sta.1) | copy-start | bytes 3076
  2.4 11.7 %collective-permute-start = (f32[640,128]{1,0:T(8,128)S(1)}, f32[640,128]{1,0:T(8,128)S(1)}, u32[]{:S(2)}, u32[]{:S(2)}) collective-permute-start(f32[640,128]{1,0:T(8,128)S(1)} %get-tuple-element.17), channel_id=1, source_target_pairs={{0,4},{4,0},{8,12},{12,8},{16,20},{20,16},{24,28},{28,24},{1,5},{5... | collective-permute-start | bytes 983048 | tf_op jit(solution)/shard_map/ppermute | solution.py:312
  3.0 22.2 %collective-permute-start.3 = (f32[640,128]{1,0:T(8,128)S(1)}, f32[640,128]{1,0:T(8,128)S(1)}, u32[]{:S(2)}, u32[]{:S(2)}) collective-permute-start(f32[640,128]{1,0:T(8,128)S(1)} %get-tuple-element.20), channel_id=1, source_target_pairs={{0,1},{1,0},{2,3},{3,2},{4,8},{5,9},{6,10},{7,11},{8,4},{9,5},{10,... | collective-permute-start | bytes 983048 | tf_op jit(solution)/shard_map/ppermute | solution.py:361
  5.5 8.6 %slice-start = ((s8[11468800]{0:T(1024)(128)(4,1)}), s8[4194304]{0:T(1024)(128)(4,1)S(1)}, s32[]{:S(2)}) async-start(s8[11468800]{0:T(1024)(128)(4,1)} %bitcast.2), calls=%async_computation | async-start | bytes 8388608
  5.5 8.6 %slice-start.1 = ((s8[11468800]{0:T(1024)(128)(4,1)}), s8[4194304]{0:T(1024)(128)(4,1)S(1)}, s32[]{:S(2)}) async-start(s8[11468800]{0:T(1024)(128)(4,1)} %bitcast.2), calls=%async_computation.1 | async-start | bytes 8388608
  5.6 8.6 %slice-start.2 = ((s8[11468800]{0:T(1024)(128)(4,1)}), s8[3080192]{0:T(1024)(128)(4,1)S(1)}, s32[]{:S(2)}) async-start(s8[11468800]{0:T(1024)(128)(4,1)} %bitcast.2), calls=%async_computation.2 | async-start | bytes 6160384
  5.6 8.6 %copy-start.1 = (f32[2,5,4,64,128]{4,3,2,1,0:T(8,128)S(1)}, f32[2,5,4,64,128]{4,3,2,1,0:T(8,128)}, u32[]{:S(2)}) copy-start(f32[2,5,4,64,128]{4,3,2,1,0:T(8,128)} %flow.3) | copy-start | bytes 3932164
  6.1 1.8 %collective-permute-start.4 = (f32[240,128]{1,0:T(8,128)S(1)}, f32[240,128]{1,0:T(8,128)S(1)}, u32[]{:S(2)}, u32[]{:S(2)}) collective-permute-start(f32[240,128]{1,0:T(8,128)S(1)} %get-tuple-element.24.sent), channel_id=1, source_target_pairs={{0,4},{4,0},{8,12},{12,8},{16,20},{20,16},{24,28},{28,24},{1,5},{5... | collective-permute-start | bytes 368648 | tf_op jit(solution)/shard_map/ppermute | solution.py:312
  6.4 4.6 %collective-permute-start.1 = (f32[10,4,128]{2,1,0:T(4,128)S(1)}, f32[10,4,128]{2,1,0:T(4,128)S(1)}, u32[]{:S(2)}, u32[]{:S(2)}) collective-permute-start(f32[10,4,128]{2,1,0:T(4,128)S(1)} %get-tuple-element.18), channel_id=1, source_target_pairs={{0,1},{1,0},{2,3},{3,2},{4,5},{5,4},{6,7},{7,6},{8,9},{9,8},{10,11... | collective-permute-start | bytes 61448 | tf_op jit(solution)/shard_map/ppermute | solution.py:312
  7.9 4.9 %collective-permute-start.2 = (f32[10,4,128]{2,1,0:T(4,128)S(1)}, f32[10,4,128]{2,1,0:T(4,128)S(1)}, u32[]{:S(2)}, u32[]{:S(2)}) collective-permute-start(f32[10,4,128]{2,1,0:T(4,128)S(1)} %get-tuple-element.19), channel_id=1, source_target_pairs={{0,4},{1,2},{2,1},{3,7},{4,0},{5,6},{6,5},{7,3},{8,12},{9,10},{10,... | collective-permute-start | bytes 61448 | tf_op jit(solution)/shard_map/ppermute | solution.py:363
  7.9 12.8 %collective-permute-start.5 = (f32[144,128]{1,0:T(8,128)S(1)}, f32[144,128]{1,0:T(8,128)S(1)}, u32[]{:S(2)}, u32[]{:S(2)}) collective-permute-start(f32[144,128]{1,0:T(8,128)S(1)} %get-tuple-element.26), channel_id=1, source_target_pairs={{0,8},{4,12},{8,0},{12,4},{16,24},{20,28},{24,16},{28,20},{1,9},{5... | collective-permute-start | bytes 221192 | tf_op jit(solution)/shard_map/ppermute | solution.py:312
  11.0 9.7 %collective-permute-start.6 = (f32[144,128]{1,0:T(8,128)S(1)}, f32[144,128]{1,0:T(8,128)S(1)}, u32[]{:S(2)}, u32[]{:S(2)}) collective-permute-start(f32[144,128]{1,0:T(8,128)S(1)} %get-tuple-element.27), channel_id=1, source_target_pairs={{0,16},{4,20},{8,24},{12,28},{16,0},{20,4},{24,8},{28,12},{1,17},{... | collective-permute-start | bytes 221192 | tf_op jit(solution)/shard_map/ppermute | solution.py:312
  12.7 8.0 %collective-permute-start.7 = (f32[144,128]{1,0:T(8,128)S(1)}, f32[144,128]{1,0:T(8,128)S(1)}, u32[]{:S(2)}, u32[]{:S(2)}) collective-permute-start(f32[144,128]{1,0:T(8,128)S(1)} %get-tuple-element.28), channel_id=1, source_target_pairs={{0,24},{4,28},{8,16},{12,20},{16,8},{20,12},{24,0},{28,4},{1,25},{... | collective-permute-start | bytes 221192 | tf_op jit(solution)/shard_map/ppermute | solution.py:312
  20.7 4.4 %copy-start.2 = (f32[5,12,12,256]{3,2,1,0:T(8,128)S(1)}, f32[5,12,12,256]{3,2,1,0:T(8,128)}, u32[]{:S(2)}) copy-start(f32[5,12,12,256]{3,2,1,0:T(8,128)} %stiff.1) | copy-start | bytes 2211844
  20.7 4.4 %copy-start.3 = (f32[5,12,4,64]{3,2,1,0:T(4,128)S(1)}, f32[5,12,4,64]{3,2,1,0:T(4,128)}, u32[]{:S(2)}) copy-start(f32[5,12,4,64]{3,2,1,0:T(4,128)} %motion.1) | copy-start | bytes 184324
  20.8 6.7 %collective-permute-start.10 = (f32[48,128]{1,0:T(8,128)S(1)}, f32[48,128]{1,0:T(8,128)S(1)}, u32[]{:S(2)}, u32[]{:S(2)}) collective-permute-start(f32[48,128]{1,0:T(8,128)S(1)} %reduce.1.rest_0_), channel_id=1, source_target_pairs={{0,3},{1,2},{2,1},{3,0},{4,7},{5,6},{6,5},{7,4},{8,11},{9,10},{10,... | collective-permute-start | bytes 73736 | tf_op jit(solution)/shard_map/ppermute | solution.py:312
  23.3 4.2 %collective-permute-start.9 = (f32[48,128]{1,0:T(8,128)S(1)}, f32[48,128]{1,0:T(8,128)S(1)}, u32[]{:S(2)}, u32[]{:S(2)}) collective-permute-start(f32[48,128]{1,0:T(8,128)S(1)} %reduce.1.rest_0_), channel_id=1, source_target_pairs={{0,2},{1,3},{2,0},{3,1},{4,6},{5,7},{6,4},{7,5},{8,10},{9,11},{10,... | collective-permute-start | bytes 73736 | tf_op jit(solution)/shard_map/ppermute | solution.py:312
  25.1 3.8 %collective-permute-start.8 = (f32[48,128]{1,0:T(8,128)S(1)}, f32[48,128]{1,0:T(8,128)S(1)}, u32[]{:S(2)}, u32[]{:S(2)}) collective-permute-start(f32[48,128]{1,0:T(8,128)S(1)} %reduce.1.rest_0_), channel_id=1, source_target_pairs={{0,1},{1,0},{2,3},{3,2},{4,5},{5,4},{6,7},{7,6},{8,9},{9,8},{10,11... | collective-permute-start | bytes 73736 | tf_op jit(solution)/shard_map/ppermute | solution.py:312

commit v2 on v1

--- a/solution.py
+++ b/solution.py
@@ -47,13 +47,11 @@
     return lane_row(sta[...] ^ (me * sta_dev), ccols)
 
 
-def face_kernel(flow, near, far, beside, across, surf):
+def face_kernel(flow, near, far, low, high, surf):
     nvec, nvar, srows, ccols, _ = flow.shape
     odd = lax.axis_index("span") % 2 == 1
     near_row = jnp.where(odd, 0, srows - 1)
     far_row = srows - 1 - near_row
-    codd = lax.axis_index("chord") % 2 == 1
-    near_col = jnp.where(codd, 0, 1)
     lane = lax.broadcasted_iota(jnp.int32, (ccols, LANES), 1)
     packed = jnp.zeros((ccols, LANES), F32)
     for v in range(nvec):
@@ -61,9 +59,8 @@
             q = v * nvar + b
             near[q * ccols : (q + 1) * ccols] = flow[v, b, near_row]
             far[q * ccols : (q + 1) * ccols] = flow[v, b, far_row]
-            low, high = flow[v, b, :, 0, :], flow[v, b, :, ccols - 1, :]
-            beside[q] = jnp.where(near_col == 0, low, high)
-            across[q] = jnp.where(near_col == 0, high, low)
+            low[q * srows : (q + 1) * srows] = flow[v, b, :, 0, :]
+            high[q * srows : (q + 1) * srows] = flow[v, b, :, ccols - 1, :]
             for r in range(srows):
                 at = q * 8 + r
                 x = flow[v, b, r]
@@ -73,13 +70,20 @@
     surf[...] = packed.T
 
 
-def pre_kernel(span, surf_in, lmap, mask, sta, beam, p1, kept, rel, maskf_out, wall):
+def neighbour_steps(chord):
+    return [m for m in range(1, chord) if m & (m + 1) == 0]
+
+
+def wall_kernel(chord, sta_dev, surf_in, lmap, mask, sta, low, high, *refs):
+    messages, (rel, maskf_out, wall) = refs[: chord - 1], refs[chord - 1 :]
+    rows = wall.shape[0]
     nvar = lmap.shape[1]
+    ndof = lmap.shape[0]
+    nvec = rows // ndof
     srows, ccols = mask.shape
-    ndof, nvec, sta_dev = beam.shape
-    k = sta_dev // LANES
-    rows = nvec * ndof
+    slab = rows * (srows * ccols // LANES)
     me = lax.axis_index("span")
+    column = lax.axis_index("chord")
     surf = surf_in[...]
     maskf = mask[...].astype(F32)
     maskf_out[...] = maskf
@@ -91,23 +95,64 @@
                 total = total + lmap[j, a] * near[a]
             wall[v * ndof + j] = total
     walls = jnp.concatenate([wall[:, r, :] for r in range(srows)], axis=1)
-    parts = halves(walls)
     stations = relative(sta, me, sta_dev, ccols)
     rel[...] = stations
-    for p in range(span):
-        both = lax.dot_general(
-            parts,
-            table(stations, p * sta_dev, sta_dev),
-            (((1,), (1,)), ((), ())),
-            preferred_element_type=F32,
-        )
-        put_slabs(p1 if p % 2 else kept, (p // 2) * rows * k, both[:rows] + both[rows:])
-    base = (span // 2) * rows * k
+    numbers = jnp.broadcast_to(stations.astype(F32), (8, stations.shape[1]))
+    for m in range(1, chord):
+        message = messages[m - 1]
+        put_slabs(message, 0, walls)
+        put_slabs(message, slab, numbers)
+        if m in neighbour_steps(chord):
+            base = slab + 8 * (walls.shape[1] // LANES)
+            message[base:] = jnp.where((column ^ m) > column, high[...], low[...])
+
+
+def dense_terms(span, first, rel, walls, rows, sta_dev, out):
+    wide = rel.shape[1] // LANES
+    k = sta_dev // LANES
+    slab = rows * wide
+    parts = [halves(get_slabs(x, 0, rows, wide)) for x in walls]
+    stations = [rel[...]]
+    for x in walls[1:]:
+        stations.append(get_slabs(x, slab, 8, wide)[:1].astype(jnp.int32))
+    for p in range(first, span, 2):
+        both = 0.0
+        for x, st in zip(parts, stations):
+            both = both + lax.dot_general(
+                x,
+                table(st, p * sta_dev, sta_dev),
+                (((1,), (1,)), ((), ())),
+                preferred_element_type=F32,
+            )
+        put_slabs(out, (p // 2) * rows * k, both[:rows] + both[rows:])
+
+
+def send_kernel(span, chord, rel, beam, *refs):
+    walls, (p1, lo, hi) = refs[:chord], refs[chord:]
+    ndof, nvec, sta_dev = beam.shape
+    k = sta_dev // LANES
+    rows = nvec * ndof
+    column = lax.axis_index("chord")
+    dense_terms(span, 1, rel, walls, rows, sta_dev, p1)
+    at0 = (span // 2) * rows * k
     for v in range(nvec):
         for j in range(ndof):
             for h in range(k):
-                at = base + h * rows + v * ndof + j
+                at = at0 + h * rows + v * ndof + j
                 p1[at : at + 1] = beam[j, v : v + 1, h * LANES : (h + 1) * LANES]
+    base = (rows + 8) * (rel.shape[1] // LANES)
+    low, high = jnp.zeros(lo.shape, F32), jnp.zeros(hi.shape, F32)
+    for m in neighbour_steps(chord):
+        x = walls[m][base:]
+        low = jnp.where((column > 0) & ((column ^ (column - 1)) == m), x, low)
+        high = jnp.where((column < chord - 1) & ((column ^ (column + 1)) == m), x, high)
+    lo[...] = low
+    hi[...] = high
+
+
+def keep_kernel(span, chord, rows, sta_dev, rel, *refs):
+    walls, kept = refs[:chord], refs[-1]
+    dense_terms(span, 0, rel, walls, rows, sta_dev, kept)
 
 
 def combine_kernel(slab, sent, got, kept, own, *out):
@@ -121,18 +166,18 @@
         o[2 * slab :] = got[base : base + slab]
 
 
-def stencil_kernel(chord, flow, jac, got, beside, across, out, near):
+def stencil_kernel(span, flow, jac, got, far, lo, hi, _, out, near, faces):
     nvec, nvar, srows, ccols, _ = flow.shape
     me = lax.axis_index("span")
     odd = me % 2
     row = lax.broadcasted_iota(jnp.int32, (ccols, LANES), 0)
     lane = lax.broadcasted_iota(jnp.int32, (ccols, LANES), 1)
-    low_on = jnp.where(odd == 1, 1.0, 0.0).astype(F32)
-    high_on = 1.0 - low_on
-    column = lax.axis_index("chord")
-    codd = column % 2
-    inner = jnp.where((column > 0) & (column < chord - 1), 1.0, 0.0).astype(F32)
+    inner = jnp.where((me > 0) & (me < span - 1), 1.0, 0.0).astype(F32)
     tile = 16
+    for q in range(nvec * nvar):
+        one, two = got[q * ccols : (q + 1) * ccols], far[q * ccols : (q + 1) * ccols] * inner
+        faces[0, q] = jnp.where(odd == 1, one, two)
+        faces[1, q] = jnp.where(odd == 1, two, one)
 
     def one_row(r, carry):
         for v in range(nvec):
@@ -140,9 +185,8 @@
                 q = v * nvar + b
                 x = flow[v, b, r]
                 left, right = pltpu.roll(x, 1, 0), pltpu.roll(x, ccols - 1, 0)
-                one, two = beside[q, pl.ds(r, 1)], across[q, pl.ds(r, 1)] * inner
-                near[0, q] = jnp.where(row == 0, jnp.where(codd == 1, one, two), left)
-                near[1, q] = jnp.where(row == ccols - 1, jnp.where(codd == 1, two, one), right)
+                near[0, q] = jnp.where(row == 0, lo[pl.ds(q * srows + r, 1)], left)
+                near[1, q] = jnp.where(row == ccols - 1, hi[pl.ds(q * srows + r, 1)], right)
                 near[2, q] = jnp.where(lane == 0, 0.0, pltpu.roll(x, 1, 1))
                 near[3, q] = jnp.where(lane == LANES - 1, 0.0, pltpu.roll(x, LANES - 1, 1))
         first, last = r == 0, r == srows - 1
@@ -161,11 +205,9 @@
                         if e == 0:
                             x = flow[v, b, r, here]
                         elif e == 1:
-                            h = got[pl.ds(q * ccols + c, tile)] * low_on
-                            x = jnp.where(first, h, flow[v, b, below, here])
+                            x = jnp.where(first, faces[0, q, here], flow[v, b, below, here])
                         elif e == 2:
-                            h = got[pl.ds(q * ccols + c, tile)] * high_on
-                            x = jnp.where(last, h, flow[v, b, above, here])
+                            x = jnp.where(last, faces[1, q, here], flow[v, b, above, here])
                         else:
                             x = near[e - 3, q, here]
                         xs.append(x)
@@ -184,21 +226,17 @@
 
 
 def couple_kernel(
-    span, flow_in, jac, far, motion, mask, rel, stiff, sent, got, *rest
+    span, flow_in, motion, mask, rel, stiff, sent, got, own_loads, *rest
 ):
     groups = span // 2
     zs = rest[: groups - 1]
-    flow, band, gath, lk = rest[groups - 1 :]
+    flow, beam_out, gath, lk = rest[groups - 1 :]
     nvec, nvar, srows, ccols, _ = flow_in.shape
     _, ndof, _, sta_dev = stiff.shape
     k = sta_dev // LANES
     rows = nvec * ndof
     slab = rows * k
     me = lax.axis_index("span")
-    odd = me % 2
-    e = 1 + odd
-    inner = jnp.where((me > 0) & (me < span - 1), 1.0, 0.0).astype(F32)
-    r_far = jnp.where(odd == 1, srows - 1, 0)
     base = groups * slab
     gath[0] = get_slabs(sent, base, rows, k)
     gath[1] = get_slabs(got, base, rows, k)
@@ -259,69 +297,31 @@
         good = (blade(other) == home) & (other >= 0) & (other < stations_all)
         x = jnp.where(good, x, 0.0)
         shifted.append([x[v * ndof : (v + 1) * ndof] for v in range(nvec)])
+    loads = own_loads[...]
+    for z in zs:
+        loads = loads + z[:slab]
+    loads = jnp.concatenate([loads[h * rows : (h + 1) * rows] for h in range(k)], axis=1)
     for i in range(ndof):
         for v in range(nvec):
             total = stiff[0, i] * shifted[0][v]
             for d in range(1, 5):
                 total = total + stiff[d, i] * shifted[d][v]
-            band[i, v : v + 1, :] = jnp.sum(total, axis=0, keepdims=True)
-    tile = 16
-
-    def body(t, carry):
-        c = pl.multiple_of(t * tile, tile)
-        here = pl.ds(c, tile)
-        acc = [[flow[v, a, r_far, here] for a in range(nvar)] for v in range(nvec)]
-        for b in range(nvar):
-            xs = [far[pl.ds((v * nvar + b) * ccols + c, tile)] * inner for v in range(nvec)]
-            for a in range(nvar):
-                m = jac[e, a, b, r_far, here].astype(F32)
-                for v in range(nvec):
-                    acc[v][a] = acc[v][a] + m * xs[v]
-        for v in range(nvec):
-            for a in range(nvar):
-                flow[v, a, r_far, here] = acc[v][a]
-        return carry
-
-    lax.fori_loop(0, ccols // tile, body, 0)
-
-
-def last_kernel(band, *rest):
-    parts, out = rest[:-1], rest[-1]
-    ndof, nvec, sta_dev = band.shape
-    rows = ndof * nvec
-    total = parts[0][...]
-    for p in parts[1:]:
-        total = total + p[...]
-    for v in range(nvec):
-        for j in range(ndof):
-            for h in range(sta_dev // LANES):
-                at = h * rows + v * ndof + j
-                cols = slice(h * LANES, (h + 1) * LANES)
-                out[j, v : v + 1, cols] = band[j, v : v + 1, cols] - total[at : at + 1]
-
-
-def reduce_kernel(_, own, *rest):
-    parts, out = rest[:-1], rest[-1]
-    total = own[...]
-    for p in parts:
-        total = total + p[: total.shape[0]]
-    out[...] = total
+            at = v * ndof + i
+            beam_out[i, v : v + 1, :] = jnp.sum(total, axis=0, keepdims=True) - loads[at : at + 1]
 
 
 def swap(x, axis, m):
     return lax.ppermute(x, axis, [(i, i ^ m) for i in range(lax.axis_size(axis))])
 
 
-def others(span, chord, along_span):
+def far_pairs(span, chord):
     pairs = []
     for i in range(span):
         for c in range(chord):
-            at, size = (i, span) if along_span else (c, chord)
-            if 0 < at < size - 1:
-                to = at + 1 if at % 2 else at - 1
-                to = (to, c) if along_span else (i, to)
+            if 0 < i < span - 1:
+                to = (i + 1 if i % 2 else i - 1, c)
             else:
-                to = (i, c ^ 1) if along_span else (i ^ 1, c)
+                to = (i, c ^ 1)
             pairs.append((i * chord + c, to[0] * chord + to[1]))
     return pairs
 
@@ -343,13 +343,13 @@
     def shape(*s):
         return jax.ShapeDtypeStruct(s, F32)
 
-    near, far, beside, across, surf = pl.pallas_call(
+    near, far, low, high, surf = pl.pallas_call(
         face_kernel,
         out_shape=(
             shape(halo, LANES),
             shape(halo, LANES),
-            shape(nq, srows, LANES),
-            shape(nq, srows, LANES),
+            shape(nq * srows, LANES),
+            shape(nq * srows, LANES),
             shape(LANES, ccols),
         ),
         in_specs=[VMEM],
@@ -358,27 +358,50 @@
         cost_estimate=pl.CostEstimate(flops=FIRST, bytes_accessed=2000000, transcendentals=0),
         name="faces",
     )(flow_state)
-    far_got = lax.ppermute(far, ("span", "chord"), others(span, chord, True))
-    beside_got = swap(beside, "chord", 1)
-    across_got = lax.ppermute(across, ("span", "chord"), others(span, chord, False))
     near_got = swap(near, "span", 1)
-
-    p1, kept, rel, maskf = pl.pallas_call(
-        functools.partial(pre_kernel, span),
+    far_got = lax.ppermute(far, ("span", "chord"), far_pairs(span, chord))
+
+    wide = srows * ccols // LANES
+    wall_rows = (rows + 8) * wide
+    message_rows = [
+        wall_rows + (nq * srows if m in neighbour_steps(chord) else 0) for m in range(1, chord)
+    ]
+    *messages, rel, maskf = pl.pallas_call(
+        functools.partial(wall_kernel, chord, sta_dev),
+        out_shape=tuple(shape(n, LANES) for n in message_rows)
+        + (jax.ShapeDtypeStruct((1, srows * ccols), jnp.int32), shape(srows, ccols)),
+        in_specs=[VMEM] * 6,
+        out_specs=(VMEM,) * (chord + 1),
+        scratch_shapes=[pltpu.VMEM((rows, srows, ccols), F32)],
+        compiler_params=params(),
+        cost_estimate=pl.CostEstimate(flops=FIRST, bytes_accessed=1000000, transcendentals=0),
+        name="wall",
+    )(surf, load_map, surface_mask, station_of, low, high)
+    wall_got = [swap(messages[m - 1], "chord", m) for m in range(1, chord)]
+
+    p1, lo, hi = pl.pallas_call(
+        functools.partial(send_kernel, span, chord),
         out_shape=(
             shape((groups + 1) * slab, LANES),
-            shape(groups * slab, LANES),
-            jax.ShapeDtypeStruct((1, srows * ccols), jnp.int32),
-            shape(srows, ccols),
+            shape(nq * srows, LANES),
+            shape(nq * srows, LANES),
         ),
-        in_specs=[VMEM] * 5,
-        out_specs=(VMEM,) * 4,
-        scratch_shapes=[pltpu.VMEM((rows, srows, ccols), F32)],
+        in_specs=[VMEM] * (chord + 2),
+        out_specs=(VMEM,) * 3,
         compiler_params=params(),
         cost_estimate=pl.CostEstimate(flops=FIRST, bytes_accessed=1000000, transcendentals=0),
-        name="pre",
-    )(surf, load_map, surface_mask, station_of, beam)
+        name="send",
+    )(rel, beam, messages[0], *wall_got)
     p1_got = swap(p1, "span", 1)
+    kept = pl.pallas_call(
+        functools.partial(keep_kernel, span, chord, rows, sta_dev),
+        out_shape=shape(groups * slab, LANES),
+        in_specs=[VMEM] * (chord + 1) + [pl.BlockSpec(memory_space=pl.ANY)],
+        out_specs=VMEM,
+        compiler_params=params(),
+        cost_estimate=pl.CostEstimate(flops=FIRST, bytes_accessed=1000000, transcendentals=0),
+        name="keep",
+    )(rel, messages[0], *wall_got, p1)
 
     own, *zs = pl.pallas_call(
         functools.partial(combine_kernel, slab),
@@ -391,11 +414,14 @@
     z_got = [swap(zs[q - 1], "span", 2 * q) for q in range(1, groups)]
 
     flow1 = pl.pallas_call(
-        functools.partial(stencil_kernel, chord),
+        functools.partial(stencil_kernel, span),
         out_shape=jax.ShapeDtypeStruct(flow_state.shape, F32),
-        in_specs=[VMEM] * 5,
+        in_specs=[VMEM] * 6 + [pl.BlockSpec(memory_space=pl.ANY)],
         out_specs=VMEM,
-        scratch_shapes=[pltpu.VMEM((4, nq, ccols, LANES), F32)],
+        scratch_shapes=[
+            pltpu.VMEM((4, nq, ccols, LANES), F32),
+            pltpu.VMEM((2, nq, ccols, LANES), F32),
+        ],
         compiler_params=params(),
         cost_estimate=pl.CostEstimate(
             flops=4 * 7 * nvar * nvar * srows * ccols * ncell,
@@ -403,22 +429,12 @@
             transcendentals=0,
         ),
         name="stencil",
-    )(flow_state, jacobians, near_got, beside_got, across_got)
-
-    loads = pl.pallas_call(
-        reduce_kernel,
-        out_shape=shape(slab, LANES),
-        in_specs=[pl.BlockSpec(memory_space=pl.ANY)] + [VMEM] * groups,
-        out_specs=VMEM,
-        compiler_params=params(),
-        name="reduce",
-    )(flow1, own, *z_got)
-    chord_got = [swap(loads, "chord", m) for m in range(1, chord)]
-
-    flow_image, band = pl.pallas_call(
+    )(flow_state, jacobians, near_got, far_got, lo, hi, own)
+
+    flow_image, out = pl.pallas_call(
         functools.partial(couple_kernel, span),
         out_shape=(jax.ShapeDtypeStruct(flow_state.shape, F32), shape(ndof, nvec, sta_dev)),
-        in_specs=[VMEM] * (9 + groups - 1),
+        in_specs=[VMEM] * (8 + groups - 1),
         out_specs=(VMEM, VMEM),
         scratch_shapes=[
             pltpu.VMEM((span, rows, sta_dev), F32),
@@ -428,17 +444,9 @@
         cost_estimate=pl.CostEstimate(flops=20000000, bytes_accessed=6000000, transcendentals=0),
         name="couple",
     )(
-        flow1, jacobians, far_got, motion_map, maskf, rel, stiffness, p1, p1_got, *z_got
+        flow1, motion_map, maskf, rel, stiffness, p1, p1_got, own, *z_got
     )
 
-    out = pl.pallas_call(
-        last_kernel,
-        out_shape=shape(ndof, nvec, sta_dev),
-        in_specs=[VMEM] * (chord + 1),
-        out_specs=VMEM,
-        compiler_params=params(),
-        name="last",
-    )(band, loads, *chord_got)
     return flow_image, jnp.transpose(out, (1, 0, 2))
 
 

time: 29.7 us -> 27 us (0.909)
  starting transfers between devices: 13.9 us -> 11 us
  waiting for transfers between devices: 2.98 us -> 2.51 us
  local copies, waits for them, and re-layouts: 1.36 us -> 1.78 us
  Pallas kernels: 10.5 us -> 10.8 us
    ppermute x9 -> x8, starting transfers between devices: 11.3 us -> 9.11 us  [swap(): lax.ppermute(x, axis, [(i, i ^ m) for i in range(lax.axis_size(axis))])]
    ppermute x2 -> x1, starting transfers between devices: 2.57 us -> 1.89 us  [on_device(): far_got = lax.ppermute(far, ('span', 'chord'), far_pairs(span, chord))]
    ppermute x9 -> x8, waiting for transfers between devices: 2.97 us -> 2.51 us  [swap(): lax.ppermute(x, axis, [(i, i ^ m) for i in range(lax.axis_size(axis))])]
    pallas_call x4, Pallas kernels: 7.71 us -> 8.16 us  [the longest x1 6.55 us: on_device(): pl.pallas_call(functools.partial(stencil_kernel, span), out_shape=jax.Sha...]
    unnamed x22, local copies, waits for them, and re-layouts: 1.36 us -> 1.78 us
  transfers between devices with their start and end apart: 11 -> 9, of which waited for: 2 -> 2; matrix products, arithmetic and copies ran while one was open for 0% -> 0% of each run, Pallas kernels for 32% -> 27%
where the time goes in v2:
time: 27 us; the launch traced here: 26.9 us
  starting transfers between devices  11 us (41%)
  Pallas kernels  10.8 us (40%)
  waiting for transfers between devices  2.51 us (9%)
  local copies, waits for them, and re-layouts  1.78 us (7%)
  between operations  0.81 us (3%)
    ppermute x8, starting transfers between devices, swap(): lax.ppermute(x, axis, [(i, i ^ m) for i in range(lax.axis_size(axis))])  9.11 us
    pallas_call x1, Pallas kernels, on_device(): pl.pallas_call(functools.partial(stencil_kernel, span), out_shape=jax.Sha...  6.55 us
    ppermute x8, waiting for transfers between devices, swap(): lax.ppermute(x, axis, [(i, i ^ m) for i in range(lax.axis_size(axis))])  2.51 us
    pallas_call x1, Pallas kernels, on_device(): pl.pallas_call(functools.partial(couple_kernel, span), out_shape=(jax.Sha...  2.11 us
    ppermute x1, starting transfers between devices, on_device(): far_got = lax.ppermute(far, ('span', 'chord'), far_pairs(span, chord))  1.89 us
    unnamed x22, local copies, waits for them, and re-layouts  1.78 us
    pallas_call x1, Pallas kernels, on_device(): pl.pallas_call(functools.partial(send_kernel, span, chord), out_shape=(sh...  0.74 us
    pallas_call x1, Pallas kernels, on_device(): pl.pallas_call(functools.partial(keep_kernel, span, chord, rows, sta_dev)...  0.73 us
  transfers between devices with their start and end apart: 9, of which 2 were waited for; matrix products, arithmetic and copies ran while one was open for 0% of the time, Pallas kernels for 27%

profile of v2, /device:TPU:0, one launch (start us, length us, event | category | flops | bytes accessed | tf_op | source)
XLA Modules:
  0.0 26.9 jit_solution(17895319205361962)
XLA Ops:
  0.6 0.0 copy-start
  0.6 1.3 %copy-done = f32[2,5,4,64,128]{4,3,2,1,0:T(8,128)S(1)} copy-done((f32[2,5,4,64,128]{4,3,2,1,0:T(8,128)S(1)}, f32[2,5,4,64,128]{4,3,2,1,0:T(8,128)}, u32[]{:S(2)}) %copy-start) | copy-done | bytes 1310744
  2.0 0.5 %faces.1 = (f32[640,128]{1,0:T(8,128)S(1)}, f32[640,128]{1,0:T(8,128)S(1)}, f32[40,128]{1,0:T(8,128)S(1)}, f32[40,128]{1,0:T(8,128)S(1)}, f32[128,64]{1,0:T(8,128)S(1)}) custom-call(f32[2,5,4,64,128]{4,3,2,1,0:T(8,128)S(1)} %copy-done), custom_call_target="tpu_custom_call" | custom-call | flops 20000000000 | bytes 2000000 | tf_op jit(solution)/shard_map/faces/pallas_call | solution.py:346
  2.4 0.4 %copy-done.4 = f32[12,5,4,64]{3,2,1,0:T(4,128)S(1)} copy-done((f32[12,5,4,64]{3,2,1,0:T(4,128)S(1)}, f32[12,5,4,64]{3,2,1,0:T(4,128)}, u32[]{:S(2)}) %copy-start.4) | copy-done | bytes 61464
  2.9 0.1 wall.1
  3.0 3.9 %collective-permute-start.4 = (f32[104,128]{1,0:T(8,128)S(1)}, f32[104,128]{1,0:T(8,128)S(1)}, u32[]{:S(2)}, u32[]{:S(2)}) collective-permute-start(f32[104,128]{1,0:T(8,128)S(1)} %get-tuple-element.29), channel_id=1, source_target_pairs={{0,3},{1,2},{2,1},{3,0},{4,7},{5,6},{6,5},{7,4},{8,11},{9,10},{10,... | collective-permute-start | bytes 159752 | tf_op jit(solution)/shard_map/ppermute | solution.py:314
  6.9 0.5 %collective-permute-start.2 = (f32[104,128]{1,0:T(8,128)S(1)}, f32[104,128]{1,0:T(8,128)S(1)}, u32[]{:S(2)}, u32[]{:S(2)}) collective-permute-start(f32[104,128]{1,0:T(8,128)S(1)} %get-tuple-element.27.refs_0_), channel_id=1, source_target_pairs={{0,1},{1,0},{2,3},{3,2},{4,5},{5,4},{6,7},{7,6},{8,9},{9,8},{10,11... | collective-permute-start | bytes 159752 | tf_op jit(solution)/shard_map/ppermute | solution.py:314
  7.5 0.1 collective-permute-start.3
  7.6 0.0 collective-permute-start
  7.6 1.9 %collective-permute-start.1 = (f32[640,128]{1,0:T(8,128)S(1)}, f32[640,128]{1,0:T(8,128)S(1)}, u32[]{:S(2)}, u32[]{:S(2)}) collective-permute-start(f32[640,128]{1,0:T(8,128)S(1)} %get-tuple-element.22), channel_id=1, source_target_pairs={{0,1},{1,0},{2,3},{3,2},{4,8},{5,9},{6,10},{7,11},{8,4},{9,5},{10,... | collective-permute-start | bytes 983048 | tf_op jit(solution)/shard_map/ppermute | solution.py:362
  9.5 1.9 %collective-permute-done.3.refs_2_ = f32[64,128]{1,0:T(8,128)S(1)} collective-permute-done((f32[64,128]{1,0:T(8,128)S(1)}, f32[64,128]{1,0:T(8,128)S(1)}, u32[]{:S(2)}, u32[]{:S(2)}) %collective-permute-start.3) | collective-permute-done | bytes 32800 | tf_op jit(solution)/shard_map/ppermute | solution.py:314
  11.4 0.7 %send.1 = (f32[240,128]{1,0:T(8,128)S(1)}, f32[40,128]{1,0:T(8,128)S(1)}, f32[40,128]{1,0:T(8,128)S(1)}) custom-call(s32[1,256]{1,0:T(1,128)S(1)} %get-tuple-element.26.rel, f32[12,2,256]{2,1,0:T(2,128)S(1)} %bitcast.4, f32[104,128]{1,0:T(8,128)S(1)} %get-tuple-element.27.refs_0_, f32[104,128]{1,0:T(8,128)S(1)} %collective-permute-done.2.refs_1_, ...), custom_call_target="tpu_custom_call" | custom-call | flops 20000000000 | bytes 1000000 | tf_op jit(solution)/shard_map/send/pallas_call | solution.py:382
  12.1 0.0 slice-start
  12.2 0.0 copy-start.1
  12.2 0.1 collective-permute-start.5
  12.3 0.7 %keep.1.kept = f32[192,128]{1,0:T(8,128)S(1)} custom-call(s32[1,256]{1,0:T(1,128)S(1)} %get-tuple-element.26.rel, f32[104,128]{1,0:T(8,128)S(1)} %get-tuple-element.27.refs_0_, f32[104,128]{1,0:T(8,128)S(1)} %collective-permute-done.2.refs_1_, f32[64,128]{1,0:T(8,128)S(1)} %collective-permute-done.3.refs_2_, f32[104,128]{1,0:T(8,128)S(1)} %collective-permute-done.4.refs_3_, ...), custom_call_target="tpu_custom_call" | custom-call | flops 20000000000 | bytes 1000000 | tf_op jit(solution)/shard_map/keep/pallas_call | solution.py:396
  13.0 0.6 %collective-permute-done.5.got = f32[240,128]{1,0:T(8,128)S(1)} collective-permute-done((f32[240,128]{1,0:T(8,128)S(1)}, f32[240,128]{1,0:T(8,128)S(1)}, u32[]{:S(2)}, u32[]{:S(2)}) %collective-permute-start.5) | collective-permute-done | bytes 122912 | tf_op jit(solution)/shard_map/ppermute | solution.py:314
  13.6 1.6 %collective-permute-start.6 = (f32[144,128]{1,0:T(8,128)S(1)}, f32[144,128]{1,0:T(8,128)S(1)}, u32[]{:S(2)}, u32[]{:S(2)}) collective-permute-start(f32[144,128]{1,0:T(8,128)S(1)} %get-tuple-element.35), channel_id=1, source_target_pairs={{0,8},{4,12},{8,0},{12,4},{16,24},{20,28},{24,16},{28,20},{1,9},{5... | collective-permute-start | bytes 221192 | tf_op jit(solution)/shard_map/ppermute | solution.py:314
  15.3 2.6 %collective-permute-start.7 = (f32[144,128]{1,0:T(8,128)S(1)}, f32[144,128]{1,0:T(8,128)S(1)}, u32[]{:S(2)}, u32[]{:S(2)}) collective-permute-start(f32[144,128]{1,0:T(8,128)S(1)} %get-tuple-element.36), channel_id=1, source_target_pairs={{0,16},{4,20},{8,24},{12,28},{16,0},{20,4},{24,8},{28,12},{1,17},{... | collective-permute-start | bytes 221192 | tf_op jit(solution)/shard_map/ppermute | solution.py:314
  17.9 0.2 collective-permute-start.8
  18.1 0.0 copy-start.2
  18.1 0.0 copy-start.3
  18.1 6.6 %stencil.1.flow_in = f32[2,5,4,64,128]{4,3,2,1,0:T(8,128)S(1)} custom-call(f32[2,5,4,64,128]{4,3,2,1,0:T(8,128)S(1)} %copy-done.1, bf16[7,5,5,4,64,128]{5,4,3,2,1,0:T(8,128)(2,1)S(1)} %bitcast.3, f32[640,128]{1,0:T(8,128)S(1)} %collective-permute-done.got, f32[640,128]{1,0:T(8,128)S(1)} %collective-permute-done.1.far, f32[40,128]{1,0:T(8,128)S(1)} %get-tuple-element.30.lo, ...), custom_call_target="tpu_custom_call" | custom-call | flops 22937600 | bytes 14090240 | tf_op jit(solution)/shard_map/stencil/pallas_call | solution.py:416
  24.8 2.1 %couple.1 = (f32[2,5,4,64,128]{4,3,2,1,0:T(8,128)}, f32[12,2,256]{2,1,0:T(2,128)}) custom-call(f32[2,5,4,64,128]{4,3,2,1,0:T(8,128)S(1)} %stencil.1.flow_in, f32[5,12,4,64]{3,2,1,0:T(4,128)S(1)} %copy-done.3, f32[4,64]{1,0:T(4,128)S(1)} %get-tuple-element.34.mask, s32[1,256]{1,0:T(1,128)S(1)} %get-tuple-element.26.rel, f32[5,12,12,256]{3,2,1,0:T(8,128)S(1)} %copy-done.2, ...), custom_call_target="tpu_custom_call" | custom-call | flops 20000000 | bytes 6000000 | tf_op jit(solution)/shard_map/couple/pallas_call | solution.py:434
  (24 shorter events, 0.1 us)
Async XLA Ops:
  0.6 1.3 %copy-start = (f32[2,5,4,64,128]{4,3,2,1,0:T(8,128)S(1)}, f32[2,5,4,64,128]{4,3,2,1,0:T(8,128)}, u32[]{:S(2)}) copy-start(f32[2,5,4,64,128]{4,3,2,1,0:T(8,128)} %flow.3) | copy-start | bytes 3932164
  1.9 0.9 %copy-start.4 = (f32[12,5,4,64]{3,2,1,0:T(4,128)S(1)}, f32[12,5,4,64]{3,2,1,0:T(4,128)}, u32[]{:S(2)}) copy-start(f32[12,5,4,64]{3,2,1,0:T(4,128)} %lmap.1) | copy-start | bytes 184324
  2.0 0.9 %copy-start.6 = (s32[4,64]{1,0:T(4,128)S(1)}, s32[4,64]{1,0:T(4,128)}, u32[]{:S(2)}) copy-start(s32[4,64]{1,0:T(4,128)} %mask.1) | copy-start | bytes 3076
  2.0 0.9 %copy-start.7 = (s32[4,64]{1,0:T(4,128)S(1)}, s32[4,64]{1,0:T(4,128)}, u32[]{:S(2)}) copy-start(s32[4,64]{1,0:T(4,128)} %sta.1) | copy-start | bytes 3076
  2.9 8.5 %copy-start.5 = (f32[2,12,256]{2,0,1:T(2,128)S(1)}, f32[2,12,256]{2,0,1:T(2,128)}, u32[]{:S(2)}) copy-start(f32[2,12,256]{2,0,1:T(2,128)} %param.10) | copy-start | bytes 73732
  3.0 8.4 %collective-permute-start.4 = (f32[104,128]{1,0:T(8,128)S(1)}, f32[104,128]{1,0:T(8,128)S(1)}, u32[]{:S(2)}, u32[]{:S(2)}) collective-permute-start(f32[104,128]{1,0:T(8,128)S(1)} %get-tuple-element.29), channel_id=1, source_target_pairs={{0,3},{1,2},{2,1},{3,0},{4,7},{5,6},{6,5},{7,4},{8,11},{9,10},{10,... | collective-permute-start | bytes 159752 | tf_op jit(solution)/shard_map/ppermute | solution.py:314
  6.9 4.5 %collective-permute-start.2 = (f32[104,128]{1,0:T(8,128)S(1)}, f32[104,128]{1,0:T(8,128)S(1)}, u32[]{:S(2)}, u32[]{:S(2)}) collective-permute-start(f32[104,128]{1,0:T(8,128)S(1)} %get-tuple-element.27.refs_0_), channel_id=1, source_target_pairs={{0,1},{1,0},{2,3},{3,2},{4,5},{5,4},{6,7},{7,6},{8,9},{9,8},{10,11... | collective-permute-start | bytes 159752 | tf_op jit(solution)/shard_map/ppermute | solution.py:314
  7.5 3.9 %collective-permute-start.3 = (f32[64,128]{1,0:T(8,128)S(1)}, f32[64,128]{1,0:T(8,128)S(1)}, u32[]{:S(2)}, u32[]{:S(2)}) collective-permute-start(f32[64,128]{1,0:T(8,128)S(1)} %get-tuple-element.28), channel_id=1, source_target_pairs={{0,2},{1,3},{2,0},{3,1},{4,6},{5,7},{6,4},{7,5},{8,10},{9,11},{10,... | collective-permute-start | bytes 98312 | tf_op jit(solution)/shard_map/ppermute | solution.py:314
  7.6 10.5 %collective-permute-start = (f32[640,128]{1,0:T(8,128)S(1)}, f32[640,128]{1,0:T(8,128)S(1)}, u32[]{:S(2)}, u32[]{:S(2)}) collective-permute-start(f32[640,128]{1,0:T(8,128)S(1)} %get-tuple-element.21), channel_id=1, source_target_pairs={{0,4},{4,0},{8,12},{12,8},{16,20},{20,16},{24,28},{28,24},{1,5},{5... | collective-permute-start | bytes 983048 | tf_op jit(solution)/shard_map/ppermute | solution.py:314
  7.6 10.5 %collective-permute-start.1 = (f32[640,128]{1,0:T(8,128)S(1)}, f32[640,128]{1,0:T(8,128)S(1)}, u32[]{:S(2)}, u32[]{:S(2)}) collective-permute-start(f32[640,128]{1,0:T(8,128)S(1)} %get-tuple-element.22), channel_id=1, source_target_pairs={{0,1},{1,0},{2,3},{3,2},{4,8},{5,9},{6,10},{7,11},{8,4},{9,5},{10,... | collective-permute-start | bytes 983048 | tf_op jit(solution)/shard_map/ppermute | solution.py:362
  12.1 5.9 %slice-start = ((s8[11468800]{0:T(1024)(128)(4,1)}), s8[4194304]{0:T(1024)(128)(4,1)S(1)}, s32[]{:S(2)}) async-start(s8[11468800]{0:T(1024)(128)(4,1)} %bitcast.2), calls=%async_computation | async-start | bytes 8388608
  12.2 5.9 %slice-start.1 = ((s8[11468800]{0:T(1024)(128)(4,1)}), s8[4194304]{0:T(1024)(128)(4,1)S(1)}, s32[]{:S(2)}) async-start(s8[11468800]{0:T(1024)(128)(4,1)} %bitcast.2), calls=%async_computation.1 | async-start | bytes 8388608
  12.2 5.9 %slice-start.2 = ((s8[11468800]{0:T(1024)(128)(4,1)}), s8[3080192]{0:T(1024)(128)(4,1)S(1)}, s32[]{:S(2)}) async-start(s8[11468800]{0:T(1024)(128)(4,1)} %bitcast.2), calls=%async_computation.2 | async-start | bytes 6160384
  12.2 5.9 %copy-start.1 = (f32[2,5,4,64,128]{4,3,2,1,0:T(8,128)S(1)}, f32[2,5,4,64,128]{4,3,2,1,0:T(8,128)}, u32[]{:S(2)}) copy-start(f32[2,5,4,64,128]{4,3,2,1,0:T(8,128)} %flow.3) | copy-start | bytes 3932164
  12.2 1.4 %collective-permute-start.5 = (f32[240,128]{1,0:T(8,128)S(1)}, f32[240,128]{1,0:T(8,128)S(1)}, u32[]{:S(2)}, u32[]{:S(2)}) collective-permute-start(f32[240,128]{1,0:T(8,128)S(1)} %get-tuple-element.32.refs_4_.sent), channel_id=1, source_target_pairs={{0,4},{4,0},{8,12},{12,8},{16,20},{20,16},{24,28},{28,24},{1,5},{5... | collective-permute-start | bytes 368648 | tf_op jit(solution)/shard_map/ppermute | solution.py:314
  13.6 11.1 %collective-permute-start.6 = (f32[144,128]{1,0:T(8,128)S(1)}, f32[144,128]{1,0:T(8,128)S(1)}, u32[]{:S(2)}, u32[]{:S(2)}) collective-permute-start(f32[144,128]{1,0:T(8,128)S(1)} %get-tuple-element.35), channel_id=1, source_target_pairs={{0,8},{4,12},{8,0},{12,4},{16,24},{20,28},{24,16},{28,20},{1,9},{5... | collective-permute-start | bytes 221192 | tf_op jit(solution)/shard_map/ppermute | solution.py:314
  15.3 9.5 %collective-permute-start.7 = (f32[144,128]{1,0:T(8,128)S(1)}, f32[144,128]{1,0:T(8,128)S(1)}, u32[]{:S(2)}, u32[]{:S(2)}) collective-permute-start(f32[144,128]{1,0:T(8,128)S(1)} %get-tuple-element.36), channel_id=1, source_target_pairs={{0,16},{4,20},{8,24},{12,28},{16,0},{20,4},{24,8},{28,12},{1,17},{... | collective-permute-start | bytes 221192 | tf_op jit(solution)/shard_map/ppermute | solution.py:314
  17.9 6.9 %collective-permute-start.8 = (f32[144,128]{1,0:T(8,128)S(1)}, f32[144,128]{1,0:T(8,128)S(1)}, u32[]{:S(2)}, u32[]{:S(2)}) collective-permute-start(f32[144,128]{1,0:T(8,128)S(1)} %get-tuple-element.37), channel_id=1, source_target_pairs={{0,24},{4,28},{8,16},{12,20},{16,8},{20,12},{24,0},{28,4},{1,25},{... | collective-permute-start | bytes 221192 | tf_op jit(solution)/shard_map/ppermute | solution.py:314
  18.1 6.6 %copy-start.2 = (f32[5,12,12,256]{3,2,1,0:T(8,128)S(1)}, f32[5,12,12,256]{3,2,1,0:T(8,128)}, u32[]{:S(2)}) copy-start(f32[5,12,12,256]{3,2,1,0:T(8,128)} %stiff.1) | copy-start | bytes 2211844
  18.1 6.6 %copy-start.3 = (f32[5,12,4,64]{3,2,1,0:T(4,128)S(1)}, f32[5,12,4,64]{3,2,1,0:T(4,128)}, u32[]{:S(2)}) copy-start(f32[5,12,4,64]{3,2,1,0:T(4,128)} %motion.1) | copy-start | bytes 184324

commit v3 on v2

--- a/solution.py
+++ b/solution.py
@@ -28,9 +28,13 @@
     return jnp.concatenate([x[r : r + 1, :width] for r in range(x.shape[0])], axis=1)
 
 
-def table(stations, first, count):
-    rows = lax.broadcasted_iota(jnp.int32, (count, stations.shape[1]), 0) + first
-    return (rows == stations).astype(F32).astype(BF16)
+def table(stations, count):
+    rows = lax.broadcasted_iota(jnp.int32, (count, stations.shape[1]), 0)
+    return (rows == (stations & (count - 1))).astype(F32).astype(BF16)
+
+
+def in_group(stations, p, count):
+    return ((stations >> (count.bit_length() - 1)) == p).astype(F32)
 
 
 def put_slabs(ref, base, rows):
@@ -115,16 +119,19 @@
     stations = [rel[...]]
     for x in walls[1:]:
         stations.append(get_slabs(x, slab, 8, wide)[:1].astype(jnp.int32))
-    for p in range(first, span, 2):
-        both = 0.0
-        for x, st in zip(parts, stations):
-            both = both + lax.dot_general(
-                x,
-                table(st, p * sta_dev, sta_dev),
-                (((1,), (1,)), ((), ())),
-                preferred_element_type=F32,
-            )
-        put_slabs(out, (p // 2) * rows * k, both[:rows] + both[rows:])
+    groups = range(first, span, 2)
+    both = 0.0
+    for x, st in zip(parts, stations):
+        spread = [x * in_group(st, p, sta_dev).astype(BF16) for p in groups]
+        both = both + lax.dot_general(
+            jnp.concatenate(spread, axis=0),
+            table(st, sta_dev),
+            (((1,), (1,)), ((), ())),
+            preferred_element_type=F32,
+        )
+    for n in range(len(groups)):
+        at = 2 * n * rows
+        put_slabs(out, n * rows * k, both[at : at + rows] + both[at + rows : at + 2 * rows])
 
 
 def send_kernel(span, chord, rel, beam, *refs):
@@ -166,14 +173,13 @@
         o[2 * slab :] = got[base : base + slab]
 
 
-def stencil_kernel(span, flow, jac, got, far, lo, hi, _, out, near, faces):
+def stencil_kernel(span, flow, jac, got, far, lo, hi, _, out, padded, faces):
     nvec, nvar, srows, ccols, _ = flow.shape
     me = lax.axis_index("span")
     odd = me % 2
-    row = lax.broadcasted_iota(jnp.int32, (ccols, LANES), 0)
-    lane = lax.broadcasted_iota(jnp.int32, (ccols, LANES), 1)
     inner = jnp.where((me > 0) & (me < span - 1), 1.0, 0.0).astype(F32)
     tile = 16
+    lane = lax.broadcasted_iota(jnp.int32, (tile, LANES), 1)
     for q in range(nvec * nvar):
         one, two = got[q * ccols : (q + 1) * ccols], far[q * ccols : (q + 1) * ccols] * inner
         faces[0, q] = jnp.where(odd == 1, one, two)
@@ -183,34 +189,36 @@
         for v in range(nvec):
             for b in range(nvar):
                 q = v * nvar + b
-                x = flow[v, b, r]
-                left, right = pltpu.roll(x, 1, 0), pltpu.roll(x, ccols - 1, 0)
-                near[0, q] = jnp.where(row == 0, lo[pl.ds(q * srows + r, 1)], left)
-                near[1, q] = jnp.where(row == ccols - 1, hi[pl.ds(q * srows + r, 1)], right)
-                near[2, q] = jnp.where(lane == 0, 0.0, pltpu.roll(x, 1, 1))
-                near[3, q] = jnp.where(lane == LANES - 1, 0.0, pltpu.roll(x, LANES - 1, 1))
+                padded[q, 8 : 8 + ccols] = flow[v, b, r]
+                padded[q, 7:8] = lo[pl.ds(q * srows + r, 1)]
+                padded[q, 8 + ccols : 9 + ccols] = hi[pl.ds(q * srows + r, 1)]
         first, last = r == 0, r == srows - 1
         below = jnp.where(first, 0, r - 1)
         above = jnp.where(last, srows - 1, r + 1)
-
-        def one_tile(t, carry):
-            c = pl.multiple_of(t * tile, tile)
-            here = pl.ds(c, tile)
+        for c in range(0, ccols, tile):
+            here = slice(c, c + tile)
+
+            def value(e, v, b):
+                q = v * nvar + b
+                if e == 1:
+                    return jnp.where(first, faces[0, q, here], flow[v, b, below, here])
+                if e == 2:
+                    return jnp.where(last, faces[1, q, here], flow[v, b, above, here])
+                if e == 3:
+                    return padded[q, c + 7 : c + 7 + tile]
+                if e == 4:
+                    return padded[q, c + 9 : c + 9 + tile]
+                x = flow[v, b, r, here]
+                if e == 5:
+                    return jnp.where(lane == 0, 0.0, pltpu.roll(x, 1, 1))
+                if e == 6:
+                    return jnp.where(lane == LANES - 1, 0.0, pltpu.roll(x, LANES - 1, 1))
+                return x
+
             acc = [[jnp.zeros((tile, LANES), F32) for _ in range(nvar)] for _ in range(nvec)]
-            for e in range(7):
-                for b in range(nvar):
-                    xs = []
-                    for v in range(nvec):
-                        q = v * nvar + b
-                        if e == 0:
-                            x = flow[v, b, r, here]
-                        elif e == 1:
-                            x = jnp.where(first, faces[0, q, here], flow[v, b, below, here])
-                        elif e == 2:
-                            x = jnp.where(last, faces[1, q, here], flow[v, b, above, here])
-                        else:
-                            x = near[e - 3, q, here]
-                        xs.append(x)
+            for b in range(nvar):
+                for e in (0, 5, 6, 1, 2, 3, 4):
+                    xs = [value(e, v, b) for v in range(nvec)]
                     for a in range(nvar):
                         m = jac[e, a, b, r, here].astype(F32)
                         for v in range(nvec):
@@ -218,9 +226,7 @@
             for v in range(nvec):
                 for a in range(nvar):
                     out[v, a, r, here] = acc[v][a]
-            return carry
-
-        return lax.fori_loop(0, ccols // tile, one_tile, carry)
+        return carry
 
     lax.fori_loop(0, srows, one_row, 0)
 
@@ -229,7 +235,7 @@
     span, flow_in, motion, mask, rel, stiff, sent, got, own_loads, *rest
 ):
     groups = span // 2
-    zs = rest[: groups - 1]
+    zs = rest[: groups - 1][::-1]
     flow, beam_out, gath, lk = rest[groups - 1 :]
     nvec, nvar, srows, ccols, _ = flow_in.shape
     _, ndof, _, sta_dev = stiff.shape
@@ -244,12 +250,13 @@
         gath[2 * q] = get_slabs(zs[q - 1], slab, rows, k)
         gath[2 * q + 1] = get_slabs(zs[q - 1], 2 * slab, rows, k)
     stations = rel[...]
-    both = jnp.zeros((2 * rows, srows * ccols), F32)
+    beams = jnp.concatenate([halves(gath[p]) for p in range(span)], axis=0)
+    each = jnp.dot(beams, table(stations, sta_dev), preferred_element_type=F32)
+    looked = jnp.zeros((rows, srows * ccols), F32)
     for p in range(span):
-        both = both + jnp.dot(
-            halves(gath[p]), table(stations, p * sta_dev, sta_dev), preferred_element_type=F32
-        )
-    looked = both[:rows] + both[rows:]
+        at = 2 * p * rows
+        both = each[at : at + rows] + each[at + rows : at + 2 * rows]
+        looked = looked + both * in_group(stations, p, sta_dev)
     for r in range(srows):
         lk[:, r, :] = looked[:, r * ccols : (r + 1) * ccols]
     maskf = mask[...]
@@ -419,7 +426,7 @@
         in_specs=[VMEM] * 6 + [pl.BlockSpec(memory_space=pl.ANY)],
         out_specs=VMEM,
         scratch_shapes=[
-            pltpu.VMEM((4, nq, ccols, LANES), F32),
+            pltpu.VMEM((nq, ccols + 16, LANES), F32),
             pltpu.VMEM((2, nq, ccols, LANES), F32),
         ],
         compiler_params=params(),
@@ -444,7 +451,7 @@
         cost_estimate=pl.CostEstimate(flops=20000000, bytes_accessed=6000000, transcendentals=0),
         name="couple",
     )(
-        flow1, motion_map, maskf, rel, stiffness, p1, p1_got, own, *z_got
+        flow1, motion_map, maskf, rel, stiffness, p1, p1_got, own, *z_got[::-1]
     )
 
     return flow_image, jnp.transpose(out, (1, 0, 2))

time: 27 us -> 25.7 us (0.952)
  Pallas kernels: 10.8 us -> 8.39 us
  waiting for transfers between devices: 2.51 us -> 3.59 us
    pallas_call x1, Pallas kernels: 6.55 us -> 4.9 us  [on_device(): pl.pallas_call(functools.partial(stencil_kernel, span), out_shape=jax.Sha...]
    ppermute x8, waiting for transfers between devices: 2.51 us -> 3.59 us  [swap(): lax.ppermute(x, axis, [(i, i ^ m) for i in range(lax.axis_size(axis))])]
    pallas_call x1, Pallas kernels: 0.74 us -> 0.37 us  [on_device(): pl.pallas_call(functools.partial(send_kernel, span, chord), out_shape=(sh...]
    pallas_call x1, Pallas kernels: 0.73 us -> 0.38 us  [on_device(): pl.pallas_call(functools.partial(keep_kernel, span, chord, rows, sta_dev)...]
  transfers between devices with their start and end apart: 9 -> 9, of which waited for: 2 -> 3; matrix products, arithmetic and copies ran while one was open for 0% -> 0% of each run, Pallas kernels for 27% -> 21%
where the time goes in v3:
time: 25.7 us; the launch traced here: 25.5 us
  starting transfers between devices  11 us (43%)
  Pallas kernels  8.39 us (33%)
  waiting for transfers between devices  3.59 us (14%)
  local copies, waits for them, and re-layouts  1.78 us (7%)
  between operations  0.78 us (3%)
    ppermute x8, starting transfers between devices, swap(): lax.ppermute(x, axis, [(i, i ^ m) for i in range(lax.axis_size(axis))])  9.11 us
    pallas_call x1, Pallas kernels, on_device(): pl.pallas_call(functools.partial(stencil_kernel, span), out_shape=jax.Sha...  4.9 us
    ppermute x8, waiting for transfers between devices, swap(): lax.ppermute(x, axis, [(i, i ^ m) for i in range(lax.axis_size(axis))])  3.59 us
    pallas_call x1, Pallas kernels, on_device(): pl.pallas_call(functools.partial(couple_kernel, span), out_shape=(jax.Sha...  2.11 us
    ppermute x1, starting transfers between devices, on_device(): far_got = lax.ppermute(far, ('span', 'chord'), far_pairs(span, chord))  1.89 us
    unnamed x22, local copies, waits for them, and re-layouts  1.78 us
  transfers between devices with their start and end apart: 9, of which 3 were waited for; matrix products, arithmetic and copies ran while one was open for 0% of the time, Pallas kernels for 21%

profile of v3, /device:TPU:0, one launch (start us, length us, event | category | flops | bytes accessed | tf_op | source)
XLA Modules:
  0.0 25.5 jit_solution(9771742067027742683)
XLA Ops:
  0.6 0.0 copy-start
  0.6 1.3 %copy-done = f32[2,5,4,64,128]{4,3,2,1,0:T(8,128)S(1)} copy-done((f32[2,5,4,64,128]{4,3,2,1,0:T(8,128)S(1)}, f32[2,5,4,64,128]{4,3,2,1,0:T(8,128)}, u32[]{:S(2)}) %copy-start) | copy-done | bytes 1310744
  2.0 0.5 %faces.1 = (f32[640,128]{1,0:T(8,128)S(1)}, f32[640,128]{1,0:T(8,128)S(1)}, f32[40,128]{1,0:T(8,128)S(1)}, f32[40,128]{1,0:T(8,128)S(1)}, f32[128,64]{1,0:T(8,128)S(1)}) custom-call(f32[2,5,4,64,128]{4,3,2,1,0:T(8,128)S(1)} %copy-done), custom_call_target="tpu_custom_call" | custom-call | flops 20000000000 | bytes 2000000 | tf_op jit(solution)/shard_map/faces/pallas_call | solution.py:353
  2.4 0.4 %copy-done.4 = f32[12,5,4,64]{3,2,1,0:T(4,128)S(1)} copy-done((f32[12,5,4,64]{3,2,1,0:T(4,128)S(1)}, f32[12,5,4,64]{3,2,1,0:T(4,128)}, u32[]{:S(2)}) %copy-start.4) | copy-done | bytes 61464
  2.9 0.1 wall.1
  3.0 3.9 %collective-permute-start.4 = (f32[104,128]{1,0:T(8,128)S(1)}, f32[104,128]{1,0:T(8,128)S(1)}, u32[]{:S(2)}, u32[]{:S(2)}) collective-permute-start(f32[104,128]{1,0:T(8,128)S(1)} %get-tuple-element.29), channel_id=1, source_target_pairs={{0,3},{1,2},{2,1},{3,0},{4,7},{5,6},{6,5},{7,4},{8,11},{9,10},{10,... | collective-permute-start | bytes 159752 | tf_op jit(solution)/shard_map/ppermute | solution.py:321
  6.9 0.5 %collective-permute-start.2 = (f32[104,128]{1,0:T(8,128)S(1)}, f32[104,128]{1,0:T(8,128)S(1)}, u32[]{:S(2)}, u32[]{:S(2)}) collective-permute-start(f32[104,128]{1,0:T(8,128)S(1)} %get-tuple-element.27.refs_0_), channel_id=1, source_target_pairs={{0,1},{1,0},{2,3},{3,2},{4,5},{5,4},{6,7},{7,6},{8,9},{9,8},{10,11... | collective-permute-start | bytes 159752 | tf_op jit(solution)/shard_map/ppermute | solution.py:321
  7.5 0.1 collective-permute-start.3
  7.6 0.0 collective-permute-start
  7.6 1.9 %collective-permute-start.1 = (f32[640,128]{1,0:T(8,128)S(1)}, f32[640,128]{1,0:T(8,128)S(1)}, u32[]{:S(2)}, u32[]{:S(2)}) collective-permute-start(f32[640,128]{1,0:T(8,128)S(1)} %get-tuple-element.22), channel_id=1, source_target_pairs={{0,1},{1,0},{2,3},{3,2},{4,8},{5,9},{6,10},{7,11},{8,4},{9,5},{10,... | collective-permute-start | bytes 983048 | tf_op jit(solution)/shard_map/ppermute | solution.py:369
  9.5 1.9 %collective-permute-done.3.refs_2_ = f32[64,128]{1,0:T(8,128)S(1)} collective-permute-done((f32[64,128]{1,0:T(8,128)S(1)}, f32[64,128]{1,0:T(8,128)S(1)}, u32[]{:S(2)}, u32[]{:S(2)}) %collective-permute-start.3) | collective-permute-done | bytes 32800 | tf_op jit(solution)/shard_map/ppermute | solution.py:321
  11.4 0.4 %send.1 = (f32[240,128]{1,0:T(8,128)S(1)}, f32[40,128]{1,0:T(8,128)S(1)}, f32[40,128]{1,0:T(8,128)S(1)}) custom-call(s32[1,256]{1,0:T(1,128)S(1)} %get-tuple-element.26.rel, f32[12,2,256]{2,1,0:T(2,128)S(1)} %bitcast.4, f32[104,128]{1,0:T(8,128)S(1)} %get-tuple-element.27.refs_0_, f32[104,128]{1,0:T(8,128)S(1)} %collective-permute-done.2.refs_1_, ...), custom_call_target="tpu_custom_call" | custom-call | flops 20000000000 | bytes 1000000 | tf_op jit(solution)/shard_map/send/pallas_call | solution.py:389
  11.8 0.0 slice-start
  11.8 0.0 copy-start.1
  11.8 0.1 collective-permute-start.5
  11.9 0.4 %keep.1.kept = f32[192,128]{1,0:T(8,128)S(1)} custom-call(s32[1,256]{1,0:T(1,128)S(1)} %get-tuple-element.26.rel, f32[104,128]{1,0:T(8,128)S(1)} %get-tuple-element.27.refs_0_, f32[104,128]{1,0:T(8,128)S(1)} %collective-permute-done.2.refs_1_, f32[64,128]{1,0:T(8,128)S(1)} %collective-permute-done.3.refs_2_, f32[104,128]{1,0:T(8,128)S(1)} %collective-permute-done.4.refs_3_, ...), custom_call_target="tpu_custom_call" | custom-call | flops 20000000000 | bytes 1000000 | tf_op jit(solution)/shard_map/keep/pallas_call | solution.py:403
  12.3 0.9 %collective-permute-done.5.got = f32[240,128]{1,0:T(8,128)S(1)} collective-permute-done((f32[240,128]{1,0:T(8,128)S(1)}, f32[240,128]{1,0:T(8,128)S(1)}, u32[]{:S(2)}, u32[]{:S(2)}) %collective-permute-start.5) | collective-permute-done | bytes 122912 | tf_op jit(solution)/shard_map/ppermute | solution.py:321
  13.3 3.7 %collective-permute-start.6 = (f32[144,128]{1,0:T(8,128)S(1)}, f32[144,128]{1,0:T(8,128)S(1)}, u32[]{:S(2)}, u32[]{:S(2)}) collective-permute-start(f32[144,128]{1,0:T(8,128)S(1)} %get-tuple-element.35), channel_id=1, source_target_pairs={{0,24},{4,28},{8,16},{12,20},{16,8},{20,12},{24,0},{28,4},{1,25},{... | collective-permute-start | bytes 221192 | tf_op jit(solution)/shard_map/ppermute | solution.py:321
  16.9 0.8 %collective-permute-start.8 = (f32[144,128]{1,0:T(8,128)S(1)}, f32[144,128]{1,0:T(8,128)S(1)}, u32[]{:S(2)}, u32[]{:S(2)}) collective-permute-start(f32[144,128]{1,0:T(8,128)S(1)} %get-tuple-element.37), channel_id=1, source_target_pairs={{0,8},{4,12},{8,0},{12,4},{16,24},{20,28},{24,16},{28,20},{1,9},{5... | collective-permute-start | bytes 221192 | tf_op jit(solution)/shard_map/ppermute | solution.py:321
  17.8 0.0 copy-start.2
  17.8 0.0 copy-start.3
  17.8 4.9 %stencil.1.flow_in = f32[2,5,4,64,128]{4,3,2,1,0:T(8,128)S(1)} custom-call(f32[2,5,4,64,128]{4,3,2,1,0:T(8,128)S(1)} %copy-done.1, bf16[7,5,5,4,64,128]{5,4,3,2,1,0:T(8,128)(2,1)S(1)} %bitcast.3, f32[640,128]{1,0:T(8,128)S(1)} %collective-permute-done.got, f32[640,128]{1,0:T(8,128)S(1)} %collective-permute-done.1.far, f32[40,128]{1,0:T(8,128)S(1)} %get-tuple-element.30.lo, ...), custom_call_target="tpu_custom_call" | custom-call | flops 22937600 | bytes 14090240 | tf_op jit(solution)/shard_map/stencil/pallas_call | solution.py:423
  22.7 0.7 %collective-permute-done.7.rest_1_ = f32[144,128]{1,0:T(8,128)S(1)} collective-permute-done((f32[144,128]{1,0:T(8,128)S(1)}, f32[144,128]{1,0:T(8,128)S(1)}, u32[]{:S(2)}, u32[]{:S(2)}) %collective-permute-start.7) | collective-permute-done | bytes 73760 | tf_op jit(solution)/shard_map/ppermute | solution.py:321
  23.4 2.1 %couple.1 = (f32[2,5,4,64,128]{4,3,2,1,0:T(8,128)}, f32[12,2,256]{2,1,0:T(2,128)}) custom-call(f32[2,5,4,64,128]{4,3,2,1,0:T(8,128)S(1)} %stencil.1.flow_in, f32[5,12,4,64]{3,2,1,0:T(4,128)S(1)} %copy-done.3, f32[4,64]{1,0:T(4,128)S(1)} %get-tuple-element.34.mask, s32[1,256]{1,0:T(1,128)S(1)} %get-tuple-element.26.rel, f32[5,12,12,256]{3,2,1,0:T(8,128)S(1)} %copy-done.2, ...), custom_call_target="tpu_custom_call" | custom-call | flops 20000000 | bytes 6000000 | tf_op jit(solution)/shard_map/couple/pallas_call | solution.py:441
  (24 shorter events, 0.1 us)
Async XLA Ops:
  0.6 1.3 %copy-start = (f32[2,5,4,64,128]{4,3,2,1,0:T(8,128)S(1)}, f32[2,5,4,64,128]{4,3,2,1,0:T(8,128)}, u32[]{:S(2)}) copy-start(f32[2,5,4,64,128]{4,3,2,1,0:T(8,128)} %flow.3) | copy-start | bytes 3932164
  1.9 0.9 %copy-start.4 = (f32[12,5,4,64]{3,2,1,0:T(4,128)S(1)}, f32[12,5,4,64]{3,2,1,0:T(4,128)}, u32[]{:S(2)}) copy-start(f32[12,5,4,64]{3,2,1,0:T(4,128)} %lmap.1) | copy-start | bytes 184324
  2.0 0.9 %copy-start.6 = (s32[4,64]{1,0:T(4,128)S(1)}, s32[4,64]{1,0:T(4,128)}, u32[]{:S(2)}) copy-start(s32[4,64]{1,0:T(4,128)} %mask.1) | copy-start | bytes 3076
  2.0 0.9 %copy-start.7 = (s32[4,64]{1,0:T(4,128)S(1)}, s32[4,64]{1,0:T(4,128)}, u32[]{:S(2)}) copy-start(s32[4,64]{1,0:T(4,128)} %sta.1) | copy-start | bytes 3076
  2.9 8.5 %copy-start.5 = (f32[2,12,256]{2,0,1:T(2,128)S(1)}, f32[2,12,256]{2,0,1:T(2,128)}, u32[]{:S(2)}) copy-start(f32[2,12,256]{2,0,1:T(2,128)} %param.10) | copy-start | bytes 73732
  3.0 8.4 %collective-permute-start.4 = (f32[104,128]{1,0:T(8,128)S(1)}, f32[104,128]{1,0:T(8,128)S(1)}, u32[]{:S(2)}, u32[]{:S(2)}) collective-permute-start(f32[104,128]{1,0:T(8,128)S(1)} %get-tuple-element.29), channel_id=1, source_target_pairs={{0,3},{1,2},{2,1},{3,0},{4,7},{5,6},{6,5},{7,4},{8,11},{9,10},{10,... | collective-permute-start | bytes 159752 | tf_op jit(solution)/shard_map/ppermute | solution.py:321
  6.9 4.5 %collective-permute-start.2 = (f32[104,128]{1,0:T(8,128)S(1)}, f32[104,128]{1,0:T(8,128)S(1)}, u32[]{:S(2)}, u32[]{:S(2)}) collective-permute-start(f32[104,128]{1,0:T(8,128)S(1)} %get-tuple-element.27.refs_0_), channel_id=1, source_target_pairs={{0,1},{1,0},{2,3},{3,2},{4,5},{5,4},{6,7},{7,6},{8,9},{9,8},{10,11... | collective-permute-start | bytes 159752 | tf_op jit(solution)/shard_map/ppermute | solution.py:321
  7.5 3.9 %collective-permute-start.3 = (f32[64,128]{1,0:T(8,128)S(1)}, f32[64,128]{1,0:T(8,128)S(1)}, u32[]{:S(2)}, u32[]{:S(2)}) collective-permute-start(f32[64,128]{1,0:T(8,128)S(1)} %get-tuple-element.28), channel_id=1, source_target_pairs={{0,2},{1,3},{2,0},{3,1},{4,6},{5,7},{6,4},{7,5},{8,10},{9,11},{10,... | collective-permute-start | bytes 98312 | tf_op jit(solution)/shard_map/ppermute | solution.py:321
  7.6 10.1 %collective-permute-start = (f32[640,128]{1,0:T(8,128)S(1)}, f32[640,128]{1,0:T(8,128)S(1)}, u32[]{:S(2)}, u32[]{:S(2)}) collective-permute-start(f32[640,128]{1,0:T(8,128)S(1)} %get-tuple-element.21), channel_id=1, source_target_pairs={{0,4},{4,0},{8,12},{12,8},{16,20},{20,16},{24,28},{28,24},{1,5},{5... | collective-permute-start | bytes 983048 | tf_op jit(solution)/shard_map/ppermute | solution.py:321
  7.6 10.1 %collective-permute-start.1 = (f32[640,128]{1,0:T(8,128)S(1)}, f32[640,128]{1,0:T(8,128)S(1)}, u32[]{:S(2)}, u32[]{:S(2)}) collective-permute-start(f32[640,128]{1,0:T(8,128)S(1)} %get-tuple-element.22), channel_id=1, source_target_pairs={{0,1},{1,0},{2,3},{3,2},{4,8},{5,9},{6,10},{7,11},{8,4},{9,5},{10,... | collective-permute-start | bytes 983048 | tf_op jit(solution)/shard_map/ppermute | solution.py:369
  11.8 5.9 %slice-start = ((s8[11468800]{0:T(1024)(128)(4,1)}), s8[4194304]{0:T(1024)(128)(4,1)S(1)}, s32[]{:S(2)}) async-start(s8[11468800]{0:T(1024)(128)(4,1)} %bitcast.2), calls=%async_computation | async-start | bytes 8388608
  11.8 5.9 %slice-start.1 = ((s8[11468800]{0:T(1024)(128)(4,1)}), s8[4194304]{0:T(1024)(128)(4,1)S(1)}, s32[]{:S(2)}) async-start(s8[11468800]{0:T(1024)(128)(4,1)} %bitcast.2), calls=%async_computation.1 | async-start | bytes 8388608
  11.8 5.9 %slice-start.2 = ((s8[11468800]{0:T(1024)(128)(4,1)}), s8[3080192]{0:T(1024)(128)(4,1)S(1)}, s32[]{:S(2)}) async-start(s8[11468800]{0:T(1024)(128)(4,1)} %bitcast.2), calls=%async_computation.2 | async-start | bytes 6160384
  11.8 5.9 %copy-start.1 = (f32[2,5,4,64,128]{4,3,2,1,0:T(8,128)S(1)}, f32[2,5,4,64,128]{4,3,2,1,0:T(8,128)}, u32[]{:S(2)}) copy-start(f32[2,5,4,64,128]{4,3,2,1,0:T(8,128)} %flow.3) | copy-start | bytes 3932164
  11.8 1.4 %collective-permute-start.5 = (f32[240,128]{1,0:T(8,128)S(1)}, f32[240,128]{1,0:T(8,128)S(1)}, u32[]{:S(2)}, u32[]{:S(2)}) collective-permute-start(f32[240,128]{1,0:T(8,128)S(1)} %get-tuple-element.32.refs_4_.sent), channel_id=1, source_target_pairs={{0,4},{4,0},{8,12},{12,8},{16,20},{20,16},{24,28},{28,24},{1,5},{5... | collective-permute-start | bytes 368648 | tf_op jit(solution)/shard_map/ppermute | solution.py:321
  13.3 9.4 %collective-permute-start.6 = (f32[144,128]{1,0:T(8,128)S(1)}, f32[144,128]{1,0:T(8,128)S(1)}, u32[]{:S(2)}, u32[]{:S(2)}) collective-permute-start(f32[144,128]{1,0:T(8,128)S(1)} %get-tuple-element.35), channel_id=1, source_target_pairs={{0,24},{4,28},{8,16},{12,20},{16,8},{20,12},{24,0},{28,4},{1,25},{... | collective-permute-start | bytes 221192 | tf_op jit(solution)/shard_map/ppermute | solution.py:321
  16.9 6.5 %collective-permute-start.7 = (f32[144,128]{1,0:T(8,128)S(1)}, f32[144,128]{1,0:T(8,128)S(1)}, u32[]{:S(2)}, u32[]{:S(2)}) collective-permute-start(f32[144,128]{1,0:T(8,128)S(1)} %get-tuple-element.36), channel_id=1, source_target_pairs={{0,16},{4,20},{8,24},{12,28},{16,0},{20,4},{24,8},{28,12},{1,17},{... | collective-permute-start | bytes 221192 | tf_op jit(solution)/shard_map/ppermute | solution.py:321
  16.9 6.5 %collective-permute-start.8 = (f32[144,128]{1,0:T(8,128)S(1)}, f32[144,128]{1,0:T(8,128)S(1)}, u32[]{:S(2)}, u32[]{:S(2)}) collective-permute-start(f32[144,128]{1,0:T(8,128)S(1)} %get-tuple-element.37), channel_id=1, source_target_pairs={{0,8},{4,12},{8,0},{12,4},{16,24},{20,28},{24,16},{28,20},{1,9},{5... | collective-permute-start | bytes 221192 | tf_op jit(solution)/shard_map/ppermute | solution.py:321
  17.8 5.7 %copy-start.2 = (f32[5,12,12,256]{3,2,1,0:T(8,128)S(1)}, f32[5,12,12,256]{3,2,1,0:T(8,128)}, u32[]{:S(2)}) copy-start(f32[5,12,12,256]{3,2,1,0:T(8,128)} %stiff.1) | copy-start | bytes 2211844
  17.8 5.7 %copy-start.3 = (f32[5,12,4,64]{3,2,1,0:T(4,128)S(1)}, f32[5,12,4,64]{3,2,1,0:T(4,128)}, u32[]{:S(2)}) copy-start(f32[5,12,4,64]{3,2,1,0:T(4,128)} %motion.1) | copy-start | bytes 184324

commit v4 on v3

--- a/solution.py
+++ b/solution.py
@@ -101,14 +101,14 @@
     walls = jnp.concatenate([wall[:, r, :] for r in range(srows)], axis=1)
     stations = relative(sta, me, sta_dev, ccols)
     rel[...] = stations
-    numbers = jnp.broadcast_to(stations.astype(F32), (8, stations.shape[1]))
+    wide = stations.shape[1] // LANES
     for m in range(1, chord):
         message = messages[m - 1]
         put_slabs(message, 0, walls)
-        put_slabs(message, slab, numbers)
+        put_slabs(message, slab, stations.astype(F32))
+        message[slab + wide : slab + 8] = jnp.zeros((8 - wide, LANES), F32)
         if m in neighbour_steps(chord):
-            base = slab + 8 * (walls.shape[1] // LANES)
-            message[base:] = jnp.where((column ^ m) > column, high[...], low[...])
+            message[slab + 8 :] = jnp.where((column ^ m) > column, high[...], low[...])
 
 
 def dense_terms(span, first, rel, walls, rows, sta_dev, out):
@@ -118,7 +118,7 @@
     parts = [halves(get_slabs(x, 0, rows, wide)) for x in walls]
     stations = [rel[...]]
     for x in walls[1:]:
-        stations.append(get_slabs(x, slab, 8, wide)[:1].astype(jnp.int32))
+        stations.append(get_slabs(x, slab, 1, wide).astype(jnp.int32))
     groups = range(first, span, 2)
     both = 0.0
     for x, st in zip(parts, stations):
@@ -147,7 +147,7 @@
             for h in range(k):
                 at = at0 + h * rows + v * ndof + j
                 p1[at : at + 1] = beam[j, v : v + 1, h * LANES : (h + 1) * LANES]
-    base = (rows + 8) * (rel.shape[1] // LANES)
+    base = rows * (rel.shape[1] // LANES) + 8
     low, high = jnp.zeros(lo.shape, F32), jnp.zeros(hi.shape, F32)
     for m in neighbour_steps(chord):
         x = walls[m][base:]
@@ -235,7 +235,8 @@
     span, flow_in, motion, mask, rel, stiff, sent, got, own_loads, *rest
 ):
     groups = span // 2
-    zs = rest[: groups - 1][::-1]
+    order = z_order(groups)
+    zs = [rest[order.index(q)] for q in range(1, groups)]
     flow, beam_out, gath, lk = rest[groups - 1 :]
     nvec, nvar, srows, ccols, _ = flow_in.shape
     _, ndof, _, sta_dev = stiff.shape
@@ -317,6 +318,11 @@
             beam_out[i, v : v + 1, :] = jnp.sum(total, axis=0, keepdims=True) - loads[at : at + 1]
 
 
+def z_order(groups):
+    half = groups // 2
+    return [q for q in range(1, groups) if q >= half] + [q for q in range(1, groups) if q < half]
+
+
 def swap(x, axis, m):
     return lax.ppermute(x, axis, [(i, i ^ m) for i in range(lax.axis_size(axis))])
 
@@ -369,7 +375,7 @@
     far_got = lax.ppermute(far, ("span", "chord"), far_pairs(span, chord))
 
     wide = srows * ccols // LANES
-    wall_rows = (rows + 8) * wide
+    wall_rows = rows * wide + 8
     message_rows = [
         wall_rows + (nq * srows if m in neighbour_steps(chord) else 0) for m in range(1, chord)
     ]
@@ -451,7 +457,7 @@
         cost_estimate=pl.CostEstimate(flops=20000000, bytes_accessed=6000000, transcendentals=0),
         name="couple",
     )(
-        flow1, motion_map, maskf, rel, stiffness, p1, p1_got, own, *z_got[::-1]
+        flow1, motion_map, maskf, rel, stiffness, p1, p1_got, own, *[z_got[q - 1] for q in z_order(groups)]
     )
 
     return flow_image, jnp.transpose(out, (1, 0, 2))

time: 25.7 us -> 25.3 us (0.984)
  transfers between devices with their start and end apart: 9 -> 9, of which waited for: 3 -> 4; matrix products, arithmetic and copies ran while one was open for 0% -> 0% of each run, Pallas kernels for 21% -> 21%
where the time goes in v4:
time: 25.3 us; the launch traced here: 25.2 us
  starting transfers between devices  10.8 us (43%)
  Pallas kernels  8.38 us (33%)
  waiting for transfers between devices  3.45 us (14%)
  local copies, waits for them, and re-layouts  1.78 us (7%)
  between operations  0.78 us (3%)
    ppermute x8, starting transfers between devices, swap(): lax.ppermute(x, axis, [(i, i ^ m) for i in range(lax.axis_size(axis))])  8.89 us
    pallas_call x1, Pallas kernels, on_device(): pl.pallas_call(functools.partial(stencil_kernel, span), out_shape=jax.Sha...  4.9 us
    ppermute x8, waiting for transfers between devices, swap(): lax.ppermute(x, axis, [(i, i ^ m) for i in range(lax.axis_size(axis))])  3.45 us
    pallas_call x1, Pallas kernels, on_device(): pl.pallas_call(functools.partial(couple_kernel, span), out_shape=(jax.Sha...  2.1 us
    ppermute x1, starting transfers between devices, on_device(): far_got = lax.ppermute(far, ('span', 'chord'), far_pairs(span, chord))  1.89 us
    unnamed x22, local copies, waits for them, and re-layouts  1.78 us
  transfers between devices with their start and end apart: 9, of which 4 were waited for; matrix products, arithmetic and copies ran while one was open for 0% of the time, Pallas kernels for 21%

profile of v4, /device:TPU:0, one launch (start us, length us, event | category | flops | bytes accessed | tf_op | source)
XLA Modules:
  0.0 25.2 jit_solution(13294115758549466431)
XLA Ops:
  0.6 0.0 copy-start
  0.6 1.3 %copy-done = f32[2,5,4,64,128]{4,3,2,1,0:T(8,128)S(1)} copy-done((f32[2,5,4,64,128]{4,3,2,1,0:T(8,128)S(1)}, f32[2,5,4,64,128]{4,3,2,1,0:T(8,128)}, u32[]{:S(2)}) %copy-start) | copy-done | bytes 1310744
  2.0 0.5 %faces.1 = (f32[640,128]{1,0:T(8,128)S(1)}, f32[640,128]{1,0:T(8,128)S(1)}, f32[40,128]{1,0:T(8,128)S(1)}, f32[40,128]{1,0:T(8,128)S(1)}, f32[128,64]{1,0:T(8,128)S(1)}) custom-call(f32[2,5,4,64,128]{4,3,2,1,0:T(8,128)S(1)} %copy-done), custom_call_target="tpu_custom_call" | custom-call | flops 20000000000 | bytes 2000000 | tf_op jit(solution)/shard_map/faces/pallas_call | solution.py:359
  2.4 0.4 %copy-done.4 = f32[12,5,4,64]{3,2,1,0:T(4,128)S(1)} copy-done((f32[12,5,4,64]{3,2,1,0:T(4,128)S(1)}, f32[12,5,4,64]{3,2,1,0:T(4,128)}, u32[]{:S(2)}) %copy-start.4) | copy-done | bytes 61464
  2.9 0.1 wall.1
  3.0 3.9 %collective-permute-start.4 = (f32[96,128]{1,0:T(8,128)S(1)}, f32[96,128]{1,0:T(8,128)S(1)}, u32[]{:S(2)}, u32[]{:S(2)}) collective-permute-start(f32[96,128]{1,0:T(8,128)S(1)} %get-tuple-element.29), channel_id=1, source_target_pairs={{0,3},{1,2},{2,1},{3,0},{4,7},{5,6},{6,5},{7,4},{8,11},{9,10},{10,... | collective-permute-start | bytes 147464 | tf_op jit(solution)/shard_map/ppermute | solution.py:327
  6.9 0.5 %collective-permute-start.2 = (f32[96,128]{1,0:T(8,128)S(1)}, f32[96,128]{1,0:T(8,128)S(1)}, u32[]{:S(2)}, u32[]{:S(2)}) collective-permute-start(f32[96,128]{1,0:T(8,128)S(1)} %get-tuple-element.27.refs_0_), channel_id=1, source_target_pairs={{0,1},{1,0},{2,3},{3,2},{4,5},{5,4},{6,7},{7,6},{8,9},{9,8},{10,11... | collective-permute-start | bytes 147464 | tf_op jit(solution)/shard_map/ppermute | solution.py:327
  7.5 0.1 collective-permute-start.3
  7.6 1.9 %collective-permute-start.1 = (f32[640,128]{1,0:T(8,128)S(1)}, f32[640,128]{1,0:T(8,128)S(1)}, u32[]{:S(2)}, u32[]{:S(2)}) collective-permute-start(f32[640,128]{1,0:T(8,128)S(1)} %get-tuple-element.22), channel_id=1, source_target_pairs={{0,1},{1,0},{2,3},{3,2},{4,8},{5,9},{6,10},{7,11},{8,4},{9,5},{10,... | collective-permute-start | bytes 983048 | tf_op jit(solution)/shard_map/ppermute | solution.py:375
  9.5 1.9 %collective-permute-done.3.refs_2_ = f32[56,128]{1,0:T(8,128)S(1)} collective-permute-done((f32[56,128]{1,0:T(8,128)S(1)}, f32[56,128]{1,0:T(8,128)S(1)}, u32[]{:S(2)}, u32[]{:S(2)}) %collective-permute-start.3) | collective-permute-done | bytes 28704 | tf_op jit(solution)/shard_map/ppermute | solution.py:327
  11.4 0.4 %send.1 = (f32[240,128]{1,0:T(8,128)S(1)}, f32[40,128]{1,0:T(8,128)S(1)}, f32[40,128]{1,0:T(8,128)S(1)}) custom-call(s32[1,256]{1,0:T(1,128)S(1)} %get-tuple-element.26.rel, f32[12,2,256]{2,1,0:T(2,128)S(1)} %bitcast.4, f32[96,128]{1,0:T(8,128)S(1)} %get-tuple-element.27.refs_0_, f32[96,128]{1,0:T(8,128)S(1)} %collective-permute-done.2.refs_1_, ...), custom_call_target="tpu_custom_call" | custom-call | flops 20000000000 | bytes 1000000 | tf_op jit(solution)/shard_map/send/pallas_call | solution.py:395
  11.7 0.0 slice-start
  11.8 0.0 copy-start.1
  11.8 0.1 collective-permute-start.5
  11.9 0.4 %keep.1.kept = f32[192,128]{1,0:T(8,128)S(1)} custom-call(s32[1,256]{1,0:T(1,128)S(1)} %get-tuple-element.26.rel, f32[96,128]{1,0:T(8,128)S(1)} %get-tuple-element.27.refs_0_, f32[96,128]{1,0:T(8,128)S(1)} %collective-permute-done.2.refs_1_, f32[56,128]{1,0:T(8,128)S(1)} %collective-permute-done.3.refs_2_, f32[96,128]{1,0:T(8,128)S(1)} %collective-permute-done.4.refs_3_, ...), custom_call_target="tpu_custom_call" | custom-call | flops 20000000000 | bytes 1000000 | tf_op jit(solution)/shard_map/keep/pallas_call | solution.py:409
  12.2 0.9 %collective-permute-done.5.got = f32[240,128]{1,0:T(8,128)S(1)} collective-permute-done((f32[240,128]{1,0:T(8,128)S(1)}, f32[240,128]{1,0:T(8,128)S(1)}, u32[]{:S(2)}, u32[]{:S(2)}) %collective-permute-start.5) | collective-permute-done | bytes 122912 | tf_op jit(solution)/shard_map/ppermute | solution.py:327
  13.2 2.7 %collective-permute-start.6 = (f32[144,128]{1,0:T(8,128)S(1)}, f32[144,128]{1,0:T(8,128)S(1)}, u32[]{:S(2)}, u32[]{:S(2)}) collective-permute-start(f32[144,128]{1,0:T(8,128)S(1)} %get-tuple-element.35), channel_id=1, source_target_pairs={{0,16},{4,20},{8,24},{12,28},{16,0},{20,4},{24,8},{28,12},{1,17},{... | collective-permute-start | bytes 221192 | tf_op jit(solution)/shard_map/ppermute | solution.py:327
  15.9 1.3 %collective-permute-start.7 = (f32[144,128]{1,0:T(8,128)S(1)}, f32[144,128]{1,0:T(8,128)S(1)}, u32[]{:S(2)}, u32[]{:S(2)}) collective-permute-start(f32[144,128]{1,0:T(8,128)S(1)} %get-tuple-element.36), channel_id=1, source_target_pairs={{0,24},{4,28},{8,16},{12,20},{16,8},{20,12},{24,0},{28,4},{1,25},{... | collective-permute-start | bytes 221192 | tf_op jit(solution)/shard_map/ppermute | solution.py:327
  17.2 0.2 collective-permute-start.8
  17.5 0.0 copy-start.2
  17.5 4.9 %stencil.1.flow_in = f32[2,5,4,64,128]{4,3,2,1,0:T(8,128)S(1)} custom-call(f32[2,5,4,64,128]{4,3,2,1,0:T(8,128)S(1)} %copy-done.1, bf16[7,5,5,4,64,128]{5,4,3,2,1,0:T(8,128)(2,1)S(1)} %bitcast.3, f32[640,128]{1,0:T(8,128)S(1)} %collective-permute-done.got, f32[640,128]{1,0:T(8,128)S(1)} %collective-permute-done.1.far, f32[40,128]{1,0:T(8,128)S(1)} %get-tuple-element.30.lo, ...), custom_call_target="tpu_custom_call" | custom-call | flops 22937600 | bytes 14090240 | tf_op jit(solution)/shard_map/stencil/pallas_call | solution.py:429
  22.4 0.1 collective-permute-done.7.rest_1_
  22.5 0.5 %collective-permute-done.8.rest_2_ = f32[144,128]{1,0:T(8,128)S(1)} collective-permute-done((f32[144,128]{1,0:T(8,128)S(1)}, f32[144,128]{1,0:T(8,128)S(1)}, u32[]{:S(2)}, u32[]{:S(2)}) %collective-permute-start.8) | collective-permute-done | bytes 73760 | tf_op jit(solution)/shard_map/ppermute | solution.py:327
  23.1 2.1 %couple.1 = (f32[2,5,4,64,128]{4,3,2,1,0:T(8,128)}, f32[12,2,256]{2,1,0:T(2,128)}) custom-call(f32[2,5,4,64,128]{4,3,2,1,0:T(8,128)S(1)} %stencil.1.flow_in, f32[5,12,4,64]{3,2,1,0:T(4,128)S(1)} %copy-done.3, f32[4,64]{1,0:T(4,128)S(1)} %get-tuple-element.34.mask, s32[1,256]{1,0:T(1,128)S(1)} %get-tuple-element.26.rel, f32[5,12,12,256]{3,2,1,0:T(8,128)S(1)} %copy-done.2, ...), custom_call_target="tpu_custom_call" | custom-call | flops 20000000 | bytes 6000000 | tf_op jit(solution)/shard_map/couple/pallas_call | solution.py:447
  (24 shorter events, 0.1 us)
Async XLA Ops:
  0.6 1.3 %copy-start = (f32[2,5,4,64,128]{4,3,2,1,0:T(8,128)S(1)}, f32[2,5,4,64,128]{4,3,2,1,0:T(8,128)}, u32[]{:S(2)}) copy-start(f32[2,5,4,64,128]{4,3,2,1,0:T(8,128)} %flow.3) | copy-start | bytes 3932164
  1.9 0.9 %copy-start.4 = (f32[12,5,4,64]{3,2,1,0:T(4,128)S(1)}, f32[12,5,4,64]{3,2,1,0:T(4,128)}, u32[]{:S(2)}) copy-start(f32[12,5,4,64]{3,2,1,0:T(4,128)} %lmap.1) | copy-start | bytes 184324
  2.0 0.9 %copy-start.6 = (s32[4,64]{1,0:T(4,128)S(1)}, s32[4,64]{1,0:T(4,128)}, u32[]{:S(2)}) copy-start(s32[4,64]{1,0:T(4,128)} %mask.1) | copy-start | bytes 3076
  2.0 0.9 %copy-start.7 = (s32[4,64]{1,0:T(4,128)S(1)}, s32[4,64]{1,0:T(4,128)}, u32[]{:S(2)}) copy-start(s32[4,64]{1,0:T(4,128)} %sta.1) | copy-start | bytes 3076
  2.9 8.5 %copy-start.5 = (f32[2,12,256]{2,0,1:T(2,128)S(1)}, f32[2,12,256]{2,0,1:T(2,128)}, u32[]{:S(2)}) copy-start(f32[2,12,256]{2,0,1:T(2,128)} %param.10) | copy-start | bytes 73732
  3.0 8.4 %collective-permute-start.4 = (f32[96,128]{1,0:T(8,128)S(1)}, f32[96,128]{1,0:T(8,128)S(1)}, u32[]{:S(2)}, u32[]{:S(2)}) collective-permute-start(f32[96,128]{1,0:T(8,128)S(1)} %get-tuple-element.29), channel_id=1, source_target_pairs={{0,3},{1,2},{2,1},{3,0},{4,7},{5,6},{6,5},{7,4},{8,11},{9,10},{10,... | collective-permute-start | bytes 147464 | tf_op jit(solution)/shard_map/ppermute | solution.py:327
  6.9 4.4 %collective-permute-start.2 = (f32[96,128]{1,0:T(8,128)S(1)}, f32[96,128]{1,0:T(8,128)S(1)}, u32[]{:S(2)}, u32[]{:S(2)}) collective-permute-start(f32[96,128]{1,0:T(8,128)S(1)} %get-tuple-element.27.refs_0_), channel_id=1, source_target_pairs={{0,1},{1,0},{2,3},{3,2},{4,5},{5,4},{6,7},{7,6},{8,9},{9,8},{10,11... | collective-permute-start | bytes 147464 | tf_op jit(solution)/shard_map/ppermute | solution.py:327
  7.5 3.9 %collective-permute-start.3 = (f32[56,128]{1,0:T(8,128)S(1)}, f32[56,128]{1,0:T(8,128)S(1)}, u32[]{:S(2)}, u32[]{:S(2)}) collective-permute-start(f32[56,128]{1,0:T(8,128)S(1)} %get-tuple-element.28), channel_id=1, source_target_pairs={{0,2},{1,3},{2,0},{3,1},{4,6},{5,7},{6,4},{7,5},{8,10},{9,11},{10,... | collective-permute-start | bytes 86024 | tf_op jit(solution)/shard_map/ppermute | solution.py:327
  7.6 9.9 %collective-permute-start = (f32[640,128]{1,0:T(8,128)S(1)}, f32[640,128]{1,0:T(8,128)S(1)}, u32[]{:S(2)}, u32[]{:S(2)}) collective-permute-start(f32[640,128]{1,0:T(8,128)S(1)} %get-tuple-element.21), channel_id=1, source_target_pairs={{0,4},{4,0},{8,12},{12,8},{16,20},{20,16},{24,28},{28,24},{1,5},{5... | collective-permute-start | bytes 983048 | tf_op jit(solution)/shard_map/ppermute | solution.py:327
  7.6 9.9 %collective-permute-start.1 = (f32[640,128]{1,0:T(8,128)S(1)}, f32[640,128]{1,0:T(8,128)S(1)}, u32[]{:S(2)}, u32[]{:S(2)}) collective-permute-start(f32[640,128]{1,0:T(8,128)S(1)} %get-tuple-element.22), channel_id=1, source_target_pairs={{0,1},{1,0},{2,3},{3,2},{4,8},{5,9},{6,10},{7,11},{8,4},{9,5},{10,... | collective-permute-start | bytes 983048 | tf_op jit(solution)/shard_map/ppermute | solution.py:375
  11.7 5.7 %slice-start = ((s8[11468800]{0:T(1024)(128)(4,1)}), s8[4194304]{0:T(1024)(128)(4,1)S(1)}, s32[]{:S(2)}) async-start(s8[11468800]{0:T(1024)(128)(4,1)} %bitcast.2), calls=%async_computation | async-start | bytes 8388608
  11.7 5.7 %slice-start.1 = ((s8[11468800]{0:T(1024)(128)(4,1)}), s8[4194304]{0:T(1024)(128)(4,1)S(1)}, s32[]{:S(2)}) async-start(s8[11468800]{0:T(1024)(128)(4,1)} %bitcast.2), calls=%async_computation.1 | async-start | bytes 8388608
  11.8 5.7 %slice-start.2 = ((s8[11468800]{0:T(1024)(128)(4,1)}), s8[3080192]{0:T(1024)(128)(4,1)S(1)}, s32[]{:S(2)}) async-start(s8[11468800]{0:T(1024)(128)(4,1)} %bitcast.2), calls=%async_computation.2 | async-start | bytes 6160384
  11.8 5.7 %copy-start.1 = (f32[2,5,4,64,128]{4,3,2,1,0:T(8,128)S(1)}, f32[2,5,4,64,128]{4,3,2,1,0:T(8,128)}, u32[]{:S(2)}) copy-start(f32[2,5,4,64,128]{4,3,2,1,0:T(8,128)} %flow.3) | copy-start | bytes 3932164
  11.8 1.4 %collective-permute-start.5 = (f32[240,128]{1,0:T(8,128)S(1)}, f32[240,128]{1,0:T(8,128)S(1)}, u32[]{:S(2)}, u32[]{:S(2)}) collective-permute-start(f32[240,128]{1,0:T(8,128)S(1)} %get-tuple-element.32.refs_4_.sent), channel_id=1, source_target_pairs={{0,4},{4,0},{8,12},{12,8},{16,20},{20,16},{24,28},{28,24},{1,5},{5... | collective-permute-start | bytes 368648 | tf_op jit(solution)/shard_map/ppermute | solution.py:327
  13.2 9.2 %collective-permute-start.6 = (f32[144,128]{1,0:T(8,128)S(1)}, f32[144,128]{1,0:T(8,128)S(1)}, u32[]{:S(2)}, u32[]{:S(2)}) collective-permute-start(f32[144,128]{1,0:T(8,128)S(1)} %get-tuple-element.35), channel_id=1, source_target_pairs={{0,16},{4,20},{8,24},{12,28},{16,0},{20,4},{24,8},{28,12},{1,17},{... | collective-permute-start | bytes 221192 | tf_op jit(solution)/shard_map/ppermute | solution.py:327
  15.9 6.7 %collective-permute-start.7 = (f32[144,128]{1,0:T(8,128)S(1)}, f32[144,128]{1,0:T(8,128)S(1)}, u32[]{:S(2)}, u32[]{:S(2)}) collective-permute-start(f32[144,128]{1,0:T(8,128)S(1)} %get-tuple-element.36), channel_id=1, source_target_pairs={{0,24},{4,28},{8,16},{12,20},{16,8},{20,12},{24,0},{28,4},{1,25},{... | collective-permute-start | bytes 221192 | tf_op jit(solution)/shard_map/ppermute | solution.py:327
  17.2 5.9 %collective-permute-start.8 = (f32[144,128]{1,0:T(8,128)S(1)}, f32[144,128]{1,0:T(8,128)S(1)}, u32[]{:S(2)}, u32[]{:S(2)}) collective-permute-start(f32[144,128]{1,0:T(8,128)S(1)} %get-tuple-element.37), channel_id=1, source_target_pairs={{0,8},{4,12},{8,0},{12,4},{16,24},{20,28},{24,16},{28,20},{1,9},{5... | collective-permute-start | bytes 221192 | tf_op jit(solution)/shard_map/ppermute | solution.py:327
  17.5 5.6 %copy-start.2 = (f32[5,12,12,256]{3,2,1,0:T(8,128)S(1)}, f32[5,12,12,256]{3,2,1,0:T(8,128)}, u32[]{:S(2)}) copy-start(f32[5,12,12,256]{3,2,1,0:T(8,128)} %stiff.1) | copy-start | bytes 2211844
  17.5 5.6 %copy-start.3 = (f32[5,12,4,64]{3,2,1,0:T(4,128)S(1)}, f32[5,12,4,64]{3,2,1,0:T(4,128)}, u32[]{:S(2)}) copy-start(f32[5,12,4,64]{3,2,1,0:T(4,128)} %motion.1) | copy-start | bytes 184324
